TPU v7x, 256 devices: a whole 4x4x8 slice. The times are simulated.
256 devices in a mesh: gx: 16 (over x, y_hi, core), gy: 16 (over z, y_lo).
Axes of the slice: x: 4, y: 4 (y_hi: 2, y_lo: 2; y = y_hi * 2 + y_lo), z: 8, core: 2. Of those that a mesh axis runs over, the one named last changes fastest.
Arguments:
- fields: float32 [4, 5, 4096, 4096], P(None, None, 'gx', 'gy'), may hold values from -40 to 40, as said below
- sea_mask: int32 [4096, 4096], P('gx', 'gy'), may hold values 0 or 1
- diffusivity: float32 [4096, 4096], P('gx', 'gy'), may hold values from 0.02 to 0.2
- coriolis: float32 [4096, 4096], P('gx', 'gy'), may hold values from 0.05 to 0.3
- nudge_weight: float32 [4, 5], replicated, may hold values from 0.3 to 0.9
- parent_modes: float32 [4, 5, 128, 128], P(None, None, 'gx', 'gy'), may hold values from -96 to 96
Outputs:
- new_fields: float32 [4, 5, 4096, 4096], P(None, None, 'gx', 'gy')
Inputs may be any that keep to these rules, and one draw needn't show every extreme that they name: `fields`: each field and level is of order one with some large-scale content.
All inputs are finite; a program needn't handle non-finite values. No bound on the sum of `sea_mask` on one device may be relied on, other than what follows from the above.
Results may differ from a plain program's by a relative error of at most 0.00005.
Values sent between devices are 32-bit elements; how exact they have to be, the bound alone decides.
A program may use at most 64 MiB of HBM per device.

v0:
```python
import math

import jax
import jax.numpy as jnp
from jax import lax
from jax.sharding import PartitionSpec as P


def padded_2(array, sides, width):
    for axis, dim in sides:
        size, length = (lax.axis_size(axis), array.shape[dim])
        up = [(i, (i + 1) % size) for i in range(size - 1)]
        down = [(j, i) for i, j in up]
        last = lax.slice_in_dim(array, length - width, length, axis=dim)
        leading = lax.slice_in_dim(array, 0, width, axis=dim)
        before = lax.ppermute(last, axis, up)
        after = lax.ppermute(leading, axis, down)
        array = jnp.concatenate([before, array, after], axis=dim)
    return array


def basis_rows(start, rows, count, modes):
    half = modes // 2
    pos = (start + jnp.arange(rows, dtype=jnp.int32))[:, None]
    freq_cos = jnp.arange(half, dtype=jnp.int32)[None, :]
    freq_sin = freq_cos + 1
    ang_cos = 2.0 * math.pi / count * (pos * freq_cos % count).astype(jnp.float32)
    ang_sin = 2.0 * math.pi / count * (pos * freq_sin % count).astype(jnp.float32)
    scale_cos = jnp.where(freq_cos == 0, math.sqrt(1.0 / count), math.sqrt(2.0 / count)).astype(
        jnp.float32
    )
    cosine = jnp.cos(ang_cos) * scale_cos
    sine = jnp.sin(ang_sin) * math.sqrt(2.0 / count)
    return jnp.concatenate([cosine, sine], axis=1)


def whole_parent(parent_modes):
    columns = lax.all_gather(parent_modes, "gx", axis=2, tiled=True)
    return lax.all_gather(columns, "gy", axis=3, tiled=True)


def body(fields, sea_mask, diffusivity, coriolis, nudge_weight, parent_modes):
    high = lax.Precision.HIGHEST
    tile_x = fields.shape[2]
    tile_y = fields.shape[3]
    count_x = tile_x * lax.axis_size("gx")
    count_y = tile_y * lax.axis_size("gy")
    modes = parent_modes.shape[2] * lax.axis_size("gx")
    ocean = sea_mask.astype(jnp.float32)
    kmask = diffusivity * ocean
    padded = padded_2(jnp.stack([kmask, ocean]), (("gx", 1), ("gy", 2)), 1)
    pk = padded[0]
    pm = padded[1]
    east = 0.5 * (kmask * pm[2:, 1:-1] + ocean * pk[2:, 1:-1])
    west = 0.5 * (kmask * pm[:-2, 1:-1] + ocean * pk[:-2, 1:-1])
    north = 0.5 * (kmask * pm[1:-1, 2:] + ocean * pk[1:-1, 2:])
    south = 0.5 * (kmask * pm[1:-1, :-2] + ocean * pk[1:-1, :-2])
    pq = padded_2(fields, (("gx", 2), ("gy", 3)), 1)
    lap = east * (pq[:, :, 2:, 1:-1] - fields) + west * (pq[:, :, :-2, 1:-1] - fields)
    lap = lap + north * (pq[:, :, 1:-1, 2:] - fields) + south * (pq[:, :, 1:-1, :-2] - fields)
    moved = fields + lap
    turned = jnp.stack(
        [moved[0], moved[1], moved[2] + coriolis * fields[3], moved[3] - coriolis * fields[2]]
    )
    stepped = ocean * turned
    basis_x = basis_rows(lax.axis_index("gx") * tile_x, tile_x, count_x, modes)
    basis_y = basis_rows(lax.axis_index("gy") * tile_y, tile_y, count_y, modes)
    left = jnp.einsum(
        "flxy,xa->flay", stepped, basis_x, precision=high, preferred_element_type=jnp.float32
    )
    partial_modes = jnp.einsum(
        "flay,yb->flab", left, basis_y, precision=high, preferred_element_type=jnp.float32
    )
    summed = lax.psum(partial_modes, ("gx", "gy"))
    gap = whole_parent(parent_modes) - summed
    right = jnp.einsum(
        "flab,yb->flay", gap, basis_y, precision=high, preferred_element_type=jnp.float32
    )
    correction = jnp.einsum(
        "xa,flay->flxy", basis_x, right, precision=high, preferred_element_type=jnp.float32
    )
    return stepped + nudge_weight[:, :, None, None] * ocean * correction


def solution(mesh):
    in_specs = (
        P(None, None, "gx", "gy"),
        P("gx", "gy"),
        P("gx", "gy"),
        P("gx", "gy"),
        P(),
        P(None, None, "gx", "gy"),
    )
    out_specs = P(None, None, "gx", "gy")
    return jax.shard_map(body, mesh=mesh, in_specs=in_specs, out_specs=out_specs, check_vma=False)
```

profile of v0, /device:TPU:1, one launch (start us, length us, event | category | flops | bytes accessed | tf_op | source)
XLA Modules:
  0.0 403.4 jit_solution(4801597396878571033)
XLA Ops:
  7.4 1.0 fusion.62
  8.4 1.1 fusion.59
  9.4 6.2 %collective-permute-start = (f32[2,1,256]{2,1,0:T(1,128)S(1)}, f32[2,1,256]{2,1,0:T(1,128)S(1)}, u32[]{:S(2)}, u32[]{:S(2)}) collective-permute-start(f32[2,1,256]{2,1,0:T(1,128)S(1)} %get-tuple-element.19), channel_id=1, source_target_pairs={{0,16},{16,32},{32,48},{48,64},{64,80},{80,96},{96,112},{112,128},... | collective-permute-start | bytes 6152 | tf_op jit(solution)/shard_map/ppermute | solution.py:16
  15.7 1.9 collective-permute-start.1
  17.6 1.0 fusion.60
  18.6 1.9 collective-permute-start.4
  20.6 0.6 copy.91
  21.2 5.1 %collective-permute-start.5 = (f32[4,5,1,256]{3,0,2,1:T(4,128)}, f32[4,5,1,256]{3,0,2,1:T(4,128)S(1)}, u32[]{:S(2)}, u32[]{:S(2)}) collective-permute-start(f32[4,5,1,256]{3,0,2,1:T(4,128)} %copy.91), channel_id=1, source_target_pairs={{0,16},{16,32},{32,48},{48,64},{64,80},{80,96},{96,112},{112,128},... | collective-permute-start | bytes 61448 | tf_op jit(solution)/shard_map/ppermute | solution.py:16
  26.3 0.9 copy.72
  27.2 28.0 %all_gather.6 = f32[4,5,128,8]{3,0,1,2:T(4,128)S(1)} all-gather(f32[4,5,8,8]{3,0,1,2:T(4,128)S(1)} %copy.72), channel_id=1, replica_groups=mesh['gx'=16,'gy'=16] {'gx'}, dimensions={2}, use_global_device_ids=true | all-gather | bytes 87040 | tf_op jit(solution)/shard_map/all_gather | solution.py:38
  55.2 1.1 copy.73
  56.2 0.0 all-gather.2.cloned.1.call-update
  56.3 0.0 all-reduce.2.cloned.1.call-start
  56.4 0.1 fusion.61
  56.6 1.5 collective-permute-start.2
  58.1 1.3 collective-permute-start.3
  59.4 1.7 fusion.33
  61.1 5.9 %copy.68 = f32[4,5,256,256]{2,3,1,0:T(8,128)} copy(f32[4,5,256,256]{3,2,1,0:T(8,128)} %param.6) | data formatting | bytes 10485760 | tf_op args[0]
  67.0 0.8 copy.69
  67.8 0.9 copy.50
  68.7 1.0 collective-permute-done.3
  69.7 0.4 pad_maximum_fusion.8
  70.1 0.1 slice_bitcast_fusion.1
  70.1 0.8 copy.54
  70.9 2.3 copy.58
  73.3 2.0 pad_maximum_fusion.12
  75.2 1.3 collective-permute-start.6
  76.5 5.6 %collective-permute-start.7 = (f32[4,5,258,1]{2,3,1,0:T(1,128)S(1)}, f32[4,5,258,1]{2,3,1,0:T(1,128)S(1)}, u32[]{:S(2)}, u32[]{:S(2)}) collective-permute-start(f32[4,5,258,1]{2,3,1,0:T(1,128)S(1)} %get-tuple-element.8), channel_id=1, source_target_pairs={{0,1},{1,2},{2,3},{3,4},{4,5},{5,6},{6,7},{7,8},{8,9},{9,10},{10,1... | collective-permute-start | bytes 61928 | tf_op jit(solution)/shard_map/ppermute | solution.py:16
  82.1 0.5 fusion.28
  82.6 0.1 copy.51
  82.8 0.1 copy.56
  82.9 0.1 copy.61
  83.1 0.1 copy.66
  83.2 18.9 %fusion.3 = f32[4,5,256,256]{2,3,1,0:T(8,128)S(1)} fusion(f32[4,5,256,256]{2,3,1,0:T(8,128)} %copy.68, f32[4,5,258,1]{2,3,1,0:T(1,128)S(1)} %collective-permute-done.7, f32[4,5,1,256]{2,3,1,0:T(8,128)} %copy-done, f32[4,5,1,256]{2,3,1,0:T(8,128)} %copy.58, f32[4,5,258,1]{2,3,1,0:T(1,128)S(1)} %collective-permute-done.6, f32[256,256]{0,1:T(8,128)S(1)} %copy.66, ...), kind=kLoop, calls=%fused_computation.4 | loop fusion | flops 26214400 | bytes 11616576 | tf_op jit(solution)/shard_map/add | solution.py:61
  102.1 0.2 slice.126
  102.3 0.7 copy-done.10
  103.1 0.4 fusion.18
  103.5 0.7 copy-done.7
  104.2 0.0 copy-done.11
  104.2 5.4 %fusion.13 = f32[128,4,5,256]{3,0,2,1:T(8,128)S(1)} fusion(f32[1,5,256,256]{2,3,1,0:T(8,128)S(1)} %get-tuple-element.6, f32[1,5,256,256]{2,3,1,0:T(8,128)S(1)} %get-tuple-element.5, f32[2,5,256,256]{2,3,1,0:T(8,128)S(1)} %slice.126, f32[256,256]{0,1:T(8,128)S(1)} %copy-done.7, f32[256,64]{0,1:T(8,128)S(1)} %copy-done.11, f32[256,64]{0,1:T(8,128)S(1)} %get-tuple-element.25), kind=kOutput, calls=%fused_computation.23 | convolution fusion | flops 2017230848 | bytes 8257536 | tf_op jit(solution)/shard_map/flxy,xa->flay/dot_general | solution.py:68
  109.7 3.3 fusion.14
  113.1 0.0 all-reduce.2.cloned.1.call-update
  113.1 9.4 %all-gather.2.cloned.1.call-done = f32[4,5,128,128]{2,0,1,3:T(4,128)} async-done(((f32[4,5,128,8]{2,0,1,3:T(4,128)}), f32[4,5,128,128]{2,0,1,3:T(4,128)}) %all-gather.2.cloned.1.call-update) | async-done | bytes 1310736 | tf_op jit(solution)/shard_map/all_gather | solution.py:39
  122.5 2.5 copy.76
  125.0 254.7 %all-reduce.2.cloned.1.call-done = f32[4,5,128,128]{3,2,1,0:T(8,128)} async-done(((f32[4,5,128,128]{3,2,1,0:T(8,128)}), f32[4,5,128,128]{3,2,1,0:T(8,128)}) %all-reduce.2.cloned.1.call-update) | async-done | bytes 1310736 | tf_op jit(solution)/shard_map/psum | solution.py:74
  379.8 4.1 %fusion.19 = f32[4,5,128,256]{2,3,1,0:T(8,128)S(1)} fusion(f32[4,5,128,128]{3,2,1,0:T(8,128)} %copy.76, f32[4,5,128,128]{3,2,1,0:T(8,128)} %all-reduce.2.cloned.1.call-done, f32[256,64]{0,1:T(8,128)S(1)} %copy-done.12, f32[256,64]{0,1:T(8,128)S(1)} %copy-done.13), kind=kOutput, calls=%fused_computation.31 | convolution fusion | flops 1006993408 | bytes 5373952 | tf_op jit(solution)/shard_map/flab,yb->flay/dot_general | solution.py:76
  383.9 6.2 %fusion.12 = f32[4,5,256,256]{2,3,1,0:T(8,128)} fusion(f32[1,5,256,256]{2,3,1,0:T(8,128)S(1)} %copy-done.6, f32[1,5,256,256]{2,3,1,0:T(8,128)S(1)} %copy-done.4, f32[2,5,256,256]{2,3,1,0:T(8,128)S(1)} %copy-done.2, f32[4,5]{1,0:T(4,128)S(1)} %copy-done.15, f32[256,256]{0,1:T(8,128)S(1)} %copy-done.7, f32[4,5,128,256]{2,3,1,0:T(8,128)S(1)} %fusion.19, ...), kind=kOutput, calls=%fused_computation.22 | convolution fusion | flops 2021163008 | bytes 13500496 | tf_op jit(solution)/shard_map/xa,flay->flxy/dot_general | solution.py:79
  390.1 5.9 %copy.80 = f32[4,5,256,256]{3,2,1,0:T(8,128)} copy(f32[4,5,256,256]{2,3,1,0:T(8,128)} %fusion.12) | data formatting | bytes 10485760 | tf_op jit(solution)/shard_map/add | solution.py:82
  (48 shorter events, 0.2 us)
Async XLA Ops:
  7.4 115.2 %all-gather.2.cloned.1.call-start = ((), (), s32[]{:S(2)}) async-start(), calls=%async_computation | async-start | bytes 1392640 | tf_op jit(solution)/shard_map/all_gather | solution.py:39
  9.4 46.9 %collective-permute-start = (f32[2,1,256]{2,1,0:T(1,128)S(1)}, f32[2,1,256]{2,1,0:T(1,128)S(1)}, u32[]{:S(2)}, u32[]{:S(2)}) collective-permute-start(f32[2,1,256]{2,1,0:T(1,128)S(1)} %get-tuple-element.19), channel_id=1, source_target_pairs={{0,16},{16,32},{32,48},{48,64},{64,80},{80,96},{96,112},{112,128},... | collective-permute-start | bytes 6152 | tf_op jit(solution)/shard_map/ppermute | solution.py:16
  15.7 40.7 %collective-permute-start.1 = (f32[2,1,256]{2,1,0:T(1,128)S(1)}, f32[2,1,256]{2,1,0:T(1,128)S(1)}, u32[]{:S(2)}, u32[]{:S(2)}) collective-permute-start(f32[2,1,256]{2,1,0:T(1,128)S(1)} %get-tuple-element.20), channel_id=1, source_target_pairs={{16,0},{32,16},{48,32},{64,48},{80,64},{96,80},{112,96},{128,112},... | collective-permute-start | bytes 6152 | tf_op jit(solution)/shard_map/ppermute | solution.py:17
  18.6 51.5 %collective-permute-start.4 = (f32[4,5,1,256]{3,0,2,1:T(4,128)S(1)}, f32[4,5,1,256]{3,0,2,1:T(4,128)S(1)}, u32[]{:S(2)}, u32[]{:S(2)}) collective-permute-start(f32[4,5,1,256]{3,0,2,1:T(4,128)S(1)} %copy.90), channel_id=1, source_target_pairs={{16,0},{32,16},{48,32},{64,48},{80,64},{96,80},{112,96},{128,112},... | collective-permute-start | bytes 61448 | tf_op jit(solution)/shard_map/ppermute | solution.py:17
  21.2 49.8 %collective-permute-start.5 = (f32[4,5,1,256]{3,0,2,1:T(4,128)}, f32[4,5,1,256]{3,0,2,1:T(4,128)S(1)}, u32[]{:S(2)}, u32[]{:S(2)}) collective-permute-start(f32[4,5,1,256]{3,0,2,1:T(4,128)} %copy.91), channel_id=1, source_target_pairs={{0,16},{16,32},{32,48},{48,64},{64,80},{80,96},{96,112},{112,128},... | collective-permute-start | bytes 61448 | tf_op jit(solution)/shard_map/ppermute | solution.py:16
  56.3 323.5 %all-reduce.2.cloned.1.call-start = ((), (), s32[]{:S(2)}) async-start(), calls=%async_computation.1 | async-start | bytes 2621440 | tf_op jit(solution)/shard_map/psum | solution.py:74
  56.6 12.1 %collective-permute-start.2 = (f32[2,258,1]{2,1,0:T(8,128)S(1)}, f32[2,258,1]{2,1,0:T(8,128)S(1)}, u32[]{:S(2)}, u32[]{:S(2)}) collective-permute-start(f32[2,258,1]{2,1,0:T(8,128)S(1)} %get-tuple-element.17), channel_id=1, source_target_pairs={{0,1},{1,2},{2,3},{3,4},{4,5},{5,6},{6,7},{7,8},{8,9},{9,10},{10,1... | collective-permute-start | bytes 6200 | tf_op jit(solution)/shard_map/ppermute | solution.py:16
  58.1 11.6 %collective-permute-start.3 = (f32[2,258,1]{2,1,0:T(8,128)S(1)}, f32[2,258,1]{2,1,0:T(8,128)S(1)}, u32[]{:S(2)}, u32[]{:S(2)}) collective-permute-start(f32[2,258,1]{2,1,0:T(8,128)S(1)} %get-tuple-element.18), channel_id=1, source_target_pairs={{1,0},{2,1},{3,2},{4,3},{5,4},{6,5},{7,6},{8,7},{9,8},{10,9},{11,1... | collective-permute-start | bytes 6200 | tf_op jit(solution)/shard_map/ppermute | solution.py:17
  61.1 5.9 %copy-start.14 = (f32[256,256]{1,0:T(8,128)S(1)}, f32[256,256]{1,0:T(8,128)}, u32[]{:S(2)}) copy-start(f32[256,256]{1,0:T(8,128)} %param.9) | copy-start | bytes 786436
  70.9 4.3 %copy-start = (f32[4,5,1,256]{2,3,1,0:T(8,128)}, f32[4,5,1,256]{2,3,1,0:T(8,128)S(1)}, u32[]{:S(2)}) copy-start(f32[4,5,1,256]{2,3,1,0:T(8,128)S(1)} %copy.54) | copy-start | bytes 61444
  73.2 8.9 %copy-start.8 = (s32[256,256]{1,0:T(8,128)S(1)}, s32[256,256]{1,0:T(8,128)}, u32[]{:S(2)}) copy-start(s32[256,256]{1,0:T(8,128)} %param.7) | copy-start | bytes 786436
  73.2 8.9 %copy-start.9 = (f32[256,256]{1,0:T(8,128)S(1)}, f32[256,256]{1,0:T(8,128)}, u32[]{:S(2)}) copy-start(f32[256,256]{1,0:T(8,128)} %param.8) | copy-start | bytes 786436
  75.2 8.0 %collective-permute-start.6 = (f32[4,5,258,1]{2,3,1,0:T(1,128)}, f32[4,5,258,1]{2,3,1,0:T(1,128)S(1)}, u32[]{:S(2)}, u32[]{:S(2)}) collective-permute-start(f32[4,5,258,1]{2,3,1,0:T(1,128)} %get-tuple-element.7), channel_id=1, source_target_pairs={{1,0},{2,1},{3,2},{4,3},{5,4},{6,5},{7,6},{8,7},{9,8},{10,9},{11,1... | collective-permute-start | bytes 61928 | tf_op jit(solution)/shard_map/ppermute | solution.py:17
  76.5 6.7 %collective-permute-start.7 = (f32[4,5,258,1]{2,3,1,0:T(1,128)S(1)}, f32[4,5,258,1]{2,3,1,0:T(1,128)S(1)}, u32[]{:S(2)}, u32[]{:S(2)}) collective-permute-start(f32[4,5,258,1]{2,3,1,0:T(1,128)S(1)} %get-tuple-element.8), channel_id=1, source_target_pairs={{0,1},{1,2},{2,3},{3,4},{4,5},{5,6},{6,7},{7,8},{8,9},{9,10},{10,1... | collective-permute-start | bytes 61928 | tf_op jit(solution)/shard_map/ppermute | solution.py:16
  83.0 19.3 %slice-start = ((s8[5242880]{0:T(1024)(128)(4,1)}), s8[1048576]{0:T(1024)(128)(4,1)S(1)}, s32[]{:S(2)}) async-start(s8[5242880]{0:T(1024)(128)(4,1)} %bitcast.28), calls=%async_computation.2 | async-start | bytes 2097152
  83.2 19.1 %slice-start.1 = ((s8[5242880]{0:T(1024)(128)(4,1)}), s8[4194304]{0:T(1024)(128)(4,1)S(1)}, s32[]{:S(2)}) async-start(s8[5242880]{0:T(1024)(128)(4,1)} %bitcast.28), calls=%async_computation.3 | async-start | bytes 8388608
  102.1 1.0 copy-start.10
  103.1 6.6 %copy-start.1 = (f32[2,5,256,256]{2,3,1,0:T(8,128)}, f32[2,5,256,256]{2,3,1,0:T(8,128)S(1)}, u32[]{:S(2)}) copy-start(f32[2,5,256,256]{2,3,1,0:T(8,128)S(1)} %slice.126) | copy-start | bytes 7864324
  103.1 1.1 copy-start.7
  103.1 1.2 copy-start.11
  103.5 6.2 %copy-start.3 = (f32[1,5,256,256]{2,3,1,0:T(8,128)}, f32[1,5,256,256]{2,3,1,0:T(8,128)S(1)}, u32[]{:S(2)}) copy-start(f32[1,5,256,256]{2,3,1,0:T(8,128)S(1)} %get-tuple-element.5) | copy-start | bytes 3932164
  103.5 6.2 %copy-start.5 = (f32[1,5,256,256]{2,3,1,0:T(8,128)}, f32[1,5,256,256]{2,3,1,0:T(8,128)S(1)}, u32[]{:S(2)}) copy-start(f32[1,5,256,256]{2,3,1,0:T(8,128)S(1)} %get-tuple-element.6) | copy-start | bytes 3932164
  103.5 6.2 %copy-start.12 = (f32[256,64]{0,1:T(8,128)S(1)}, f32[256,64]{0,1:T(8,128)}, u32[]{:S(2)}) copy-start(f32[256,64]{0,1:T(8,128)} %get-tuple-element.27) | copy-start | bytes 196612
  103.5 6.2 %copy-start.13 = (f32[256,64]{0,1:T(8,128)S(1)}, f32[256,64]{0,1:T(8,128)}, u32[]{:S(2)}) copy-start(f32[256,64]{0,1:T(8,128)} %get-tuple-element.28) | copy-start | bytes 196612
  113.0 270.8 %copy-start.2 = (f32[2,5,256,256]{2,3,1,0:T(8,128)S(1)}, f32[2,5,256,256]{2,3,1,0:T(8,128)}, u32[]{:S(2)}) copy-start(f32[2,5,256,256]{2,3,1,0:T(8,128)} %copy-done.1) | copy-start | bytes 7864324
  113.1 270.8 %copy-start.15 = (f32[4,5]{1,0:T(4,128)S(1)}, f32[4,5]{1,0:T(4,128)}, u32[]{:S(2)}) copy-start(f32[4,5]{1,0:T(4,128)} %param.10) | copy-start | bytes 244
  379.8 4.1 %copy-start.4 = (f32[1,5,256,256]{2,3,1,0:T(8,128)S(1)}, f32[1,5,256,256]{2,3,1,0:T(8,128)}, u32[]{:S(2)}) copy-start(f32[1,5,256,256]{2,3,1,0:T(8,128)} %copy-done.3) | copy-start | bytes 3932164
  379.8 4.1 %copy-start.6 = (f32[1,5,256,256]{2,3,1,0:T(8,128)S(1)}, f32[1,5,256,256]{2,3,1,0:T(8,128)}, u32[]{:S(2)}) copy-start(f32[1,5,256,256]{2,3,1,0:T(8,128)} %copy-done.5) | copy-start | bytes 3932164
Sparse Core Ops, SparseCore 0:
  56.4 66.0 all-gather.1
Sparse Core Ops, SparseCore 1:
  113.2 266.5 all-reduce.1
where the time goes:
time: 405 us; the launch traced here: 403 us
  waiting for transfers between devices  265 us (65%)
  blocking collectives  28 us (7%)
  other arithmetic  25.9 us (6%)
  local copies, waits for them, and re-layouts  25.1 us (6%)
  starting transfers between devices  24.9 us (6%)
  matrix products  19 us (5%)
  between operations  15.3 us (4%)
    psum x1, waiting for transfers between devices, body(): summed = lax.psum(partial_modes, ('gx', 'gy'))  255 us
    all_gather x1, blocking collectives, whole_parent(): columns = lax.all_gather(parent_modes, 'gx', axis=2, tiled=True)  28 us
    add x1, other arithmetic, body(): moved = fields + lap  18.9 us
    ppermute x4, starting transfers between devices, padded_2(): before = lax.ppermute(last, axis, up)  18.4 us
    unnamed x41, local copies, waits for them, and re-layouts  9.82 us
    all_gather x1, waiting for transfers between devices, whole_parent(): return lax.all_gather(columns, 'gy', axis=3, tiled=True)  9.44 us
  transfers between devices with their start and end apart: 10, of which 3 were waited for; matrix products, arithmetic and copies ran while one was open for 12% of the time, Pallas kernels for 0%

commit v1 on v0

v1 whole, which is shorter than its diff:
```python
import functools
import math

import jax
import jax.numpy as jnp
import numpy as np
from jax import lax
from jax.experimental import pallas as pl
from jax.experimental.pallas import tpu as pltpu
from jax.sharding import PartitionSpec as P

MESH = pl.DeviceIdType.MESH
STRIP = 16
PAD = 8
HALO = 24


def basis_table(count, modes):
    half = modes // 2
    pos = np.arange(count, dtype=np.int64)[:, None]
    freq = np.arange(half, dtype=np.int64)[None, :]
    scale = np.where(freq == 0, math.sqrt(1.0 / count), math.sqrt(2.0 / count))
    cosine = scale * np.cos(2.0 * math.pi * (pos * freq % count) / count)
    sine = math.sqrt(2.0 / count) * np.sin(2.0 * math.pi * (pos * (freq + 1) % count) / count)
    return np.concatenate([cosine, sine], axis=1)


def basis_pair(count, modes, tiles):
    wide = basis_table(count, modes).astype(np.float32).reshape(tiles, count // tiles, modes)
    return wide, np.ascontiguousarray(np.swapaxes(wide, 1, 2))


def split(value):
    high = value.astype(jnp.bfloat16)
    low = (value - high.astype(jnp.float32)).astype(jnp.bfloat16)
    return high, low


def dot(a, b):
    return jnp.dot(a, b, preferred_element_type=jnp.float32)


def step_kernel(
    dims,
    fields, mask, diff, cor, parent, wide_y, tall_x,
    stepped, gap,
    q_s, m_s, mi_s, di_s, co_s, yf_s, xf_s, ey_s, ex_s, coef, out_s, hi_s, lo_s,
    rp, rh, cp, ch, pack, hc,
    part, core_in, mine, chip_in, row_s, rt, y_in, pt, gt, blk,
    in_sem, tab_sem, halo_send, halo_recv, out_sem,
    core_send, core_recv, chip_send, chip_recv, y_send, y_recv, g_send, g_recv,
    b_send, b_recv, f_send, f_recv, own_sem,
):
    n_gx, n_gy, n_f, n_l, tx, ty, modes = dims
    n_j = n_gx // 2
    kb = modes // n_gx
    kyb = modes // n_gy
    n_fl = n_f * n_l
    rows = n_fl * kb
    n_t = rt.shape[1]
    gx = lax.axis_index("gx")
    gy = lax.axis_index("gy")
    core = lax.rem(gx, 2)
    chip = lax.div(gx, 2)
    other = 1 - core
    partner = 2 * chip + other
    up_x, dn_x = lax.rem(gx + 1, n_gx), lax.rem(gx + n_gx - 1, n_gx)
    up_y, dn_y = lax.rem(gy + 1, n_gy), lax.rem(gy + n_gy - 1, n_gy)

    def to_x(i):
        return (i, gy)

    def to_y(i):
        return (gx, i)

    def load(l):
        return pltpu.make_async_copy(
            fields.at[:, l], q_s.at[l, :, pl.ds(PAD, tx), :], in_sem.at[l]
        )

    small = [
        pltpu.make_async_copy(mask, mi_s, tab_sem.at[0]),
        pltpu.make_async_copy(diff, di_s, tab_sem.at[1]),
        pltpu.make_async_copy(cor, co_s, tab_sem.at[2]),
        pltpu.make_async_copy(wide_y.at[gy], yf_s, tab_sem.at[3]),
        pltpu.make_async_copy(tall_x.at[gx], xf_s, tab_sem.at[4]),
    ]
    for c in small[:2]:
        c.start()
    for l in range(n_l):
        load(l).start()
    for c in small[2:]:
        c.start()

    ch[...] = jnp.zeros(ch.shape, jnp.float32)

    barrier = pltpu.get_barrier_semaphore()

    def greet(dev):
        pl.semaphore_signal(barrier, inc=1, device_id=dev, device_id_type=MESH)

    greet(to_x(up_x))
    greet(to_x(dn_x))
    greet(to_x(partner))
    lax.fori_loop(1, n_j, lambda d, c: (greet(to_x(2 * lax.rem(chip + d, n_j) + core)), c)[1], 0)
    lax.fori_loop(1, n_gy, lambda d, c: (greet(to_y(lax.rem(gy + d, n_gy))), c)[1], 0)

    lane = lax.broadcasted_iota(jnp.int32, (tx, 128), 1)
    for c in small[:2]:
        c.wait()
    m = mi_s[...].astype(jnp.float32)
    m_s[0, pl.ds(PAD, tx), :] = m
    m_s[1, pl.ds(PAD, tx), :] = di_s[...] * m
    for side in range(2):
        rp[side, pl.ds(n_fl, HALO - n_fl), :] = jnp.zeros((HALO - n_fl, ty), jnp.float32)
        at = PAD if side == 0 else PAD + tx - 1
        col = 0 if side == 0 else ty - 1
        acc = jnp.zeros((tx, 128), jnp.float32)
        for k in range(2):
            rp[side, n_fl + k : n_fl + k + 1, :] = m_s[k, at : at + 1, :]
            edge = jnp.broadcast_to(m_s[k, PAD : PAD + tx, col : col + 1], (tx, 128))
            acc = jnp.where(lane == n_fl + k, edge, acc)
        pack[side] = acc

    def pack_level(l, carry):
        load(l).wait()
        for side in range(2):
            at = PAD if side == 0 else PAD + tx - 1
            col = 0 if side == 0 else ty - 1
            acc = pack[side]
            for f in range(n_f):
                rp[side, pl.ds(l * n_f + f, 1), :] = q_s[l, f, at : at + 1, :]
                edge = jnp.broadcast_to(q_s[l, f, PAD : PAD + tx, col : col + 1], (tx, 128))
                acc = jnp.where(lane == l * n_f + f, edge, acc)
            pack[side] = acc
        return carry

    lax.fori_loop(0, n_l, pack_level, 0)
    for side in range(2):
        cp[side] = pack[side].T[:HALO]

    pl.semaphore_wait(barrier, 3 + (n_j - 1) + (n_gy - 1))

    def halo_copy(k):
        src, dst, dev = [
            (rp.at[0], rh.at[1], to_x(dn_x)),
            (rp.at[1], rh.at[0], to_x(up_x)),
            (cp.at[0], ch.at[1, pl.ds(0, HALO), :], to_y(dn_y)),
            (cp.at[1], ch.at[0, pl.ds(0, HALO), :], to_y(up_y)),
        ][k]
        return pltpu.make_async_remote_copy(
            src_ref=src, dst_ref=dst, send_sem=halo_send.at[k], recv_sem=halo_recv.at[k],
            device_id=dev, device_id_type=MESH,
        )

    for k in range(4):
        halo_copy(k).start()

    for c in small[2:]:
        c.wait()
    ey_s[:, :modes], ey_s[:, modes:] = split(yf_s[...])
    ex_s[:modes, :], ex_s[modes:, :] = split(xf_s[...])
    pack_rows = n_t * 128
    blk[...] = jnp.zeros((pack_rows, 128), jnp.float32)
    for f in range(n_f):
        for l in range(n_l):
            blk[pl.ds((l * n_f + f) * kb, kb), pl.ds(0, kyb)] = parent[f, l]
    for t in range(n_t):
        pt[t] = blk[t * 128 : (t + 1) * 128, :].T[:kyb]
    row_s[...] = jnp.zeros((pack_rows, 128), jnp.float32)

    for k in range(4):
        halo_copy(k).wait_recv()

    has = [
        (gx > 0).astype(jnp.float32),
        (gx < n_gx - 1).astype(jnp.float32),
        (gy > 0).astype(jnp.float32),
        (gy < n_gy - 1).astype(jnp.float32),
    ]
    for side in range(2):
        at = PAD - 1 if side == 0 else PAD + tx
        for k in range(2):
            m_s[k, at : at + 1, :] = rh[side, n_fl + k : n_fl + k + 1, :] * has[side]

        def put(l, carry, side=side, at=at):
            for f in range(n_f):
                q_s[l, f, at : at + 1, :] = rh[side, pl.ds(l * n_f + f, 1), :]
            return carry

        lax.fori_loop(0, n_l, put, 0)
        hc[side] = ch[side].T

    lane_s = lax.broadcasted_iota(jnp.int32, (STRIP, 128), 1)
    is_first = lane_s == 0
    is_last = lane_s == 127

    def neighbours(v, r0, slot, scale=None):
        span = STRIP + 2 * PAD
        q = v[PAD : PAD + STRIP]
        west = pltpu.roll(v, 1, 0)[PAD : PAD + STRIP]
        east = pltpu.roll(v, span - 1, 0)[PAD : PAD + STRIP]
        h_lo = pltpu.roll(hc[0, pl.ds(r0, STRIP), :], lax.rem(128 - slot, 128), 1)
        h_hi = pltpu.roll(hc[1, pl.ds(r0, STRIP), :], 127 - slot, 1)
        if scale is not None:
            h_lo, h_hi = h_lo * scale[0], h_hi * scale[1]
        south = pltpu.roll(q, 1, 1)
        north = pltpu.roll(q, ty - 1, 1)
        south = jnp.concatenate(
            [jnp.where(is_first, h_lo, south[:, :128]), south[:, 128:]], axis=1
        )
        north = jnp.concatenate(
            [north[:, : ty - 128], jnp.where(is_last, h_hi, north[:, ty - 128 :])], axis=1
        )
        return q, east, west, north, south

    def coef_strip(i, carry):
        r0 = pl.multiple_of(i * STRIP, STRIP)
        window = pl.ds(r0, STRIP + 2 * PAD)
        ms = neighbours(m_s[0, window, :], r0, n_fl, (has[2], has[3]))
        ks = neighbours(m_s[1, window, :], r0, n_fl + 1, (has[2], has[3]))
        here = pl.ds(r0, STRIP)
        total = None
        for k in range(4):
            e = 0.5 * (ks[0] * ms[1 + k] + ms[0] * ks[1 + k])
            coef[k, here, :] = ms[0] * e
            total = e if total is None else total + e
        coef[4, here, :] = ms[0] * (1.0 - total)
        coef[5, here, :] = ms[0] * co_s[here, :]
        return carry

    lax.fori_loop(0, tx // STRIP, coef_strip, 0)

    def core_copy(l):
        return pltpu.make_async_remote_copy(
            src_ref=part.at[l, other], dst_ref=core_in.at[l],
            send_sem=core_send.at[l], recv_sem=core_recv.at[l],
            device_id=to_x(partner), device_id_type=MESH,
        )

    def chip_copy(l, d):
        there = lax.rem(chip + d, n_j)
        return pltpu.make_async_remote_copy(
            src_ref=mine.at[l, there], dst_ref=chip_in.at[l, chip],
            send_sem=chip_send.at[l, there], recv_sem=chip_recv.at[l, chip],
            device_id=to_x(2 * there + core), device_id_type=MESH,
        )

    def chip_arrival(l, d):
        there = lax.rem(chip + d, n_j)
        return pltpu.make_async_remote_copy(
            src_ref=mine.at[l, there], dst_ref=chip_in.at[l, there],
            send_sem=chip_send.at[l, there], recv_sem=chip_recv.at[l, there],
            device_id=to_x(2 * there + core), device_id_type=MESH,
        )

    def out_copy(l):
        return pltpu.make_async_copy(out_s.at[l], stepped.at[l], out_sem.at[l])

    def pass_on(l):
        core_copy(l).wait_recv()
        mine[l] = part[l, core] + core_in[l]
        lax.fori_loop(1, n_j, lambda d, c: (chip_copy(l, d).start(), c)[1], 0)

    def level(l, carry):
        def strip(i, c):
            r0 = pl.multiple_of(i * STRIP, STRIP)
            here = pl.ds(r0, STRIP)
            window = pl.ds(r0, STRIP + 2 * PAD)
            ce, cw, cn, cs, cc, ck = [coef[k, here, :] for k in range(6)]
            turn = {}
            for f in range(n_f):
                q, e, w, n, s = neighbours(q_s[l, f, window, :], r0, l * n_f + f)
                value = cc * q + (ce * e + cw * w) + (cn * n + cs * s)
                if f == 2:
                    value = value + ck * q_s[l, 3, pl.ds(r0 + PAD, STRIP), :]
                if f == 3:
                    value = value - ck * q_s[l, 2, pl.ds(r0 + PAD, STRIP), :]
                out_s[l, f, here, :] = value
                hi, lo = split(value)
                hi_s[f, here, :] = hi
                lo_s[f, here, :] = lo
            return c

        lax.fori_loop(0, tx // STRIP, strip, 0)
        out_copy(l).start()
        both = dot(hi_s[...].reshape(n_f * tx, ty), ey_s[...])
        left = both[:, :modes] + both[:, modes:]
        left = left + dot(lo_s[...].reshape(n_f * tx, ty), ey_s[:, :modes])
        left_hi, left_lo = split(left)

        def beside(v):
            return jnp.concatenate([v[f * tx : (f + 1) * tx] for f in range(n_f)], axis=1)

        both = dot(ex_s[...], beside(left_hi))
        proj = both[:modes] + both[modes:] + dot(ex_s[:modes, :], beside(left_lo))
        for g in range(n_gx):
            for f in range(n_f):
                part[l, g % 2, g // 2, f] = proj[
                    g * kb : (g + 1) * kb, f * modes : (f + 1) * modes
                ]
        core_copy(l).start()

        @pl.when(l > 0)
        def _():
            pass_on(l - 1)

        return carry

    lax.fori_loop(0, n_l, level, 0)
    pass_on(n_l - 1)

    def sum_level(l, carry):
        total = mine[l, chip]

        def add(d, t):
            chip_arrival(l, d).wait_recv()
            return t + chip_in[l, lax.rem(chip + d, n_j)]

        total = lax.fori_loop(1, n_j, add, total)
        row_s[pl.ds(pl.multiple_of(l * n_f * kb, 8), n_f * kb), :] = total.reshape(n_f * kb, 128)
        return carry

    lax.fori_loop(0, n_l, sum_level, 0)
    for t in range(n_t):
        rt[:, t] = row_s[t * 128 : (t + 1) * 128, :].T.reshape(n_gy, kyb, 128)

    def y_copy(d, arrival=False):
        there = lax.rem(gy + d, n_gy)
        slot = there if arrival else gy
        return pltpu.make_async_remote_copy(
            src_ref=rt.at[there], dst_ref=y_in.at[slot],
            send_sem=y_send.at[there], recv_sem=y_recv.at[slot],
            device_id=to_y(there), device_id_type=MESH,
        )

    lax.fori_loop(1, n_gy, lambda d, c: (y_copy(d).start(), c)[1], 0)

    def y_add(d, t):
        y_copy(d, True).wait_recv()
        return t + y_in[lax.rem(gy + d, n_gy)]

    total = lax.fori_loop(1, n_gy, y_add, rt[gy])
    gt[gy] = pt[...] - total

    def g_copy(d, arrival=False):
        there = lax.rem(gy + d, n_gy)
        slot = there if arrival else gy
        return pltpu.make_async_remote_copy(
            src_ref=gt.at[gy], dst_ref=gt.at[slot],
            send_sem=g_send.at[there], recv_sem=g_recv.at[slot],
            device_id=to_y(there), device_id_type=MESH,
        )

    lax.fori_loop(1, n_gy, lambda d, c: (g_copy(d).start(), c)[1], 0)
    lax.fori_loop(1, n_gy, lambda d, c: (g_copy(d, True).wait_recv(), c)[1], 0)
    for t in range(n_t):
        blk[t * 128 : (t + 1) * 128, :] = gt[:, t].reshape(128, 128).T

    block = blk.at[pl.ds(0, rows), :]

    def b_copy(d, arrival=False):
        there = lax.rem(chip + d, n_j)
        slot = there if arrival else chip
        return pltpu.make_async_remote_copy(
            src_ref=block, dst_ref=gap.at[2 * slot + core],
            send_sem=b_send.at[there], recv_sem=b_recv.at[slot],
            device_id=to_x(2 * there + core), device_id_type=MESH,
        )

    def f_copy(j, src=None, arrival=False):
        at = gap.at[2 * j + (other if arrival else core)]
        return pltpu.make_async_remote_copy(
            src_ref=at if src is None else src, dst_ref=at,
            send_sem=f_send.at[j], recv_sem=f_recv.at[j],
            device_id=to_x(partner), device_id_type=MESH,
        )

    lax.fori_loop(1, n_j, lambda d, c: (b_copy(d).start(), c)[1], 0)
    f_copy(chip, block).start()
    own = pltpu.make_async_copy(block, gap.at[gx], own_sem)
    own.start()

    def forward(d, c):
        b_copy(d, True).wait_recv()
        f_copy(lax.rem(chip + d, n_j)).start()
        return c

    lax.fori_loop(1, n_j, forward, 0)
    lax.fori_loop(0, n_j, lambda j, c: (f_copy(j, None, True).wait_recv(), c)[1], 0)

    own.wait()
    for k in range(4):
        halo_copy(k).wait_send()

    def drain(l, c):
        out_copy(l).wait()
        core_copy(l).wait_send()
        return lax.fori_loop(1, n_j, lambda d, e: (chip_copy(l, d).wait_send(), e)[1], c)

    lax.fori_loop(0, n_l, drain, 0)

    def drain_y(d, c):
        y_copy(d).wait_send()
        g_copy(d).wait_send()
        return c

    lax.fori_loop(1, n_gy, drain_y, 0)

    def drain_x(d, c):
        b_copy(d).wait_send()
        f_copy(lax.rem(chip + d, n_j)).wait_send()
        return c

    lax.fori_loop(1, n_j, drain_x, 0)
    f_copy(chip, block).wait_send()


def synth_kernel(
    dims, stepped, gap, mask, nudge, wide_x, tall_y, out, xf_s, yf_s, ex_s, ey_s, m_s, sem
):
    n_gx, n_gy, n_f, n_l, tx, ty, modes = dims
    l = pl.program_id(0)

    @pl.when(l == 0)
    def _():
        copies = [
            pltpu.make_async_copy(wide_x.at[lax.axis_index("gx")], xf_s, sem.at[0]),
            pltpu.make_async_copy(tall_y.at[lax.axis_index("gy")], yf_s, sem.at[1]),
        ]
        for c in copies:
            c.start()
        m_s[...] = mask[...].astype(jnp.float32)
        for c in copies:
            c.wait()
        ex_s[:, :modes], ex_s[:, modes:] = split(xf_s[...])
        ey_s[:modes, :], ey_s[modes:, :] = split(yf_s[...])

    g = jnp.concatenate([gap[:, 0, f].reshape(modes, modes) for f in range(n_f)], axis=0)
    g_hi, g_lo = split(g)
    y_hi = ey_s[:modes, :]
    right = dot(g_hi, y_hi) + dot(g_lo, y_hi) + dot(g_hi, ey_s[modes:, :])
    r_hi, r_lo = split(right)
    for f in range(n_f):
        here = slice(f * modes, (f + 1) * modes)
        twice = jnp.concatenate([r_hi[here], r_hi[here]], axis=0)
        corr = dot(ex_s[...], twice) + dot(ex_s[:, :modes], r_lo[here])
        out[f, 0] = stepped[0, f] + (nudge[f, l] * m_s[...]) * corr


def body(n_gx, n_gy, fields, sea_mask, diffusivity, coriolis, nudge_weight, parent_modes):
    n_f, n_l, tx, ty = fields.shape
    modes = parent_modes.shape[2] * n_gx
    kb, kyb = modes // n_gx, modes // n_gy
    n_fl = n_f * n_l
    rows = n_fl * kb
    n_t = -(-rows // 128)
    n_j = n_gx // 2
    dims = (n_gx, n_gy, n_f, n_l, tx, ty, modes)
    wide_x, tall_x = [jnp.asarray(t) for t in basis_pair(tx * n_gx, modes, n_gx)]
    if (tx, n_gx) == (ty, n_gy):
        wide_y, tall_y = wide_x, tall_x
    else:
        wide_y, tall_y = [jnp.asarray(t) for t in basis_pair(ty * n_gy, modes, n_gy)]
    any_space = pl.BlockSpec(memory_space=pl.ANY)
    vmem = pl.BlockSpec(memory_space=pltpu.VMEM)
    f32, bf16 = jnp.float32, jnp.bfloat16
    dma = pltpu.SemaphoreType.DMA
    stepped, gap = pl.pallas_call(
        functools.partial(step_kernel, dims),
        out_shape=(
            jax.ShapeDtypeStruct((n_l, n_f, tx, ty), f32),
            jax.ShapeDtypeStruct((n_gx, rows, 128), f32),
        ),
        in_specs=[any_space] * 4 + [vmem] + [any_space] * 2,
        out_specs=(any_space, any_space),
        scratch_shapes=[
            pltpu.VMEM((n_l, n_f, tx + 2 * PAD, ty), f32),
            pltpu.VMEM((2, tx + 2 * PAD, ty), f32),
            pltpu.VMEM((tx, ty), jnp.int32),
            pltpu.VMEM((tx, ty), f32),
            pltpu.VMEM((tx, ty), f32),
            pltpu.VMEM((ty, modes), f32),
            pltpu.VMEM((modes, tx), f32),
            pltpu.VMEM((ty, 2 * modes), bf16),
            pltpu.VMEM((2 * modes, tx), bf16),
            pltpu.VMEM((6, tx, ty), f32),
            pltpu.VMEM((n_l, n_f, tx, ty), f32),
            pltpu.VMEM((n_f, tx, ty), bf16),
            pltpu.VMEM((n_f, tx, ty), bf16),
            pltpu.VMEM((2, HALO, ty), f32),
            pltpu.VMEM((2, HALO, ty), f32),
            pltpu.VMEM((2, HALO, tx), f32),
            pltpu.VMEM((2, 128, tx), f32),
            pltpu.VMEM((2, tx, 128), f32),
            pltpu.VMEM((2, tx, 128), f32),
            pltpu.VMEM((n_l, 2, n_j, n_f, kb, 128), f32),
            pltpu.VMEM((n_l, n_j, n_f, kb, 128), f32),
            pltpu.VMEM((n_l, n_j, n_f, kb, 128), f32),
            pltpu.VMEM((n_l, n_j, n_f, kb, 128), f32),
            pltpu.VMEM((n_t * 128, 128), f32),
            pltpu.VMEM((n_gy, n_t, kyb, 128), f32),
            pltpu.VMEM((n_gy, n_t, kyb, 128), f32),
            pltpu.VMEM((n_t, kyb, 128), f32),
            pltpu.VMEM((n_gy, n_t, kyb, 128), f32),
            pltpu.VMEM((n_t * 128, 128), f32),
            dma((n_l,)), dma((5,)), dma((4,)), dma((4,)), dma((n_l,)),
            dma((n_l,)), dma((n_l,)), dma((n_l, n_j)), dma((n_l, n_j)),
            dma((n_gy,)), dma((n_gy,)), dma((n_gy,)), dma((n_gy,)),
            dma((n_j,)), dma((n_j,)), dma((n_j,)), dma((n_j,)), dma,
        ],
        compiler_params=pltpu.CompilerParams(
            collective_id=0, has_side_effects=True, vmem_limit_bytes=60 * 2**20
        ),
        name="step_and_project",
    )(fields, sea_mask, diffusivity, coriolis, parent_modes, wide_y, tall_x)

    return pl.pallas_call(
        functools.partial(synth_kernel, dims),
        grid=(n_l,),
        out_shape=jax.ShapeDtypeStruct(fields.shape, f32),
        in_specs=[
            pl.BlockSpec((1, n_f, tx, ty), lambda l: (l, 0, 0, 0)),
            pl.BlockSpec((n_gx, 1, n_f, kb, 128), lambda l: (0, l, 0, 0, 0)),
            pl.BlockSpec((tx, ty), lambda l: (0, 0)),
            pl.BlockSpec(memory_space=pltpu.SMEM),
            any_space,
            any_space,
        ],
        out_specs=pl.BlockSpec((n_f, 1, tx, ty), lambda l: (0, l, 0, 0)),
        scratch_shapes=[
            pltpu.VMEM((tx, modes), f32),
            pltpu.VMEM((modes, ty), f32),
            pltpu.VMEM((tx, 2 * modes), bf16),
            pltpu.VMEM((2 * modes, ty), bf16),
            pltpu.VMEM((tx, ty), f32),
            dma((2,)),
        ],
        compiler_params=pltpu.CompilerParams(vmem_limit_bytes=60 * 2**20),
        name="synthesis",
    )(stepped, gap.reshape(n_gx, n_l, n_f, kb, 128), sea_mask, nudge_weight, wide_x, tall_y)


def solution(mesh):
    tile = P(None, None, "gx", "gy")
    flat = P("gx", "gy")
    sizes = dict(mesh.shape)
    return jax.shard_map(
        functools.partial(body, sizes["gx"], sizes["gy"]),
        mesh=mesh,
        in_specs=(tile, flat, flat, flat, P(), tile),
        out_specs=tile,
        check_vma=False,
    )
```

time: 405 us -> 73 us (0.18)
  waiting for transfers between devices: 265 us -> 0 us
  Pallas kernels: 0 us -> 72.7 us
  blocking collectives: 28 us -> 0 us
  other arithmetic: 25.9 us -> 0 us
  local copies, waits for them, and re-layouts: 25.1 us -> 0 us
  starting transfers between devices: 24.9 us -> 0 us
  matrix products: 19 us -> 0 us
  between operations: 15.3 us -> 0.01 us
    psum x1 -> x0, waiting for transfers between devices: 255 us -> none  [body(): summed = lax.psum(partial_modes, ('gx', 'gy'))]
    pallas_call x0 -> x2, Pallas kernels: none -> 72.7 us  [the longest x1 63.2 us: body(): pl.pallas_call(functools.partial(step_kernel, dims), out_shape=(jax.Shape...]
    all_gather x1 -> x0, blocking collectives: 28 us -> none  [whole_parent(): columns = lax.all_gather(parent_modes, 'gx', axis=2, tiled=True)]
    ppermute x8 -> x0, starting transfers between devices: 24.8 us -> none  [the longest x4 18.4 us: padded_2(): before = lax.ppermute(last, axis, up)]
    add x4 -> x0, other arithmetic: 19.3 us -> none  [the longest x1 18.9 us: body(): moved = fields + lap]
    dot_general x4 -> x0, matrix products: 19 us -> none  [the longest x1 6.2 us: body(): jnp.einsum('xa,flay->flxy', basis_x, right, precision=high, preferred_ele...]
    unnamed x41 -> x0, local copies, waits for them, and re-layouts: 9.82 us -> none
    all_gather x1 -> x0, waiting for transfers between devices: 9.44 us -> none  [whole_parent(): return lax.all_gather(columns, 'gy', axis=3, tiled=True)]
  transfers between devices with their start and end apart: 10 -> 0, of which waited for: 3 -> 0; matrix products, arithmetic and copies ran while one was open for 12% -> 0% of each run, Pallas kernels for 0% -> 0%
where the time goes in v1:
time: 73 us; the launch traced here: 72.7 us
  Pallas kernels  72.7 us (100%)
    pallas_call x1, Pallas kernels, body(): pl.pallas_call(functools.partial(step_kernel, dims), out_shape=(jax.Shape...  63.2 us
    pallas_call x1, Pallas kernels, body(): pl.pallas_call(functools.partial(synth_kernel, dims), grid=(n_l,), out_sh...  9.53 us

profile of v1, /device:TPU:1, one launch (start us, length us, event | category | flops | bytes accessed | tf_op | source)
XLA Modules:
  0.0 72.7 jit_solution(931441110764701469)
XLA Ops:
  0.0 63.2 %step_and_project.1 = (f32[5,4,256,256]{3,2,1,0:T(8,128)}, f32[16,160,128]{2,1,0:T(8,128)}) custom-call(f32[4,5,256,256]{3,2,1,0:T(8,128)} %fields.1, s32[256,256]{1,0:T(8,128)} %mask.3, f32[256,256]{1,0:T(8,128)} %diff.1, f32[256,256]{1,0:T(8,128)} %cor.1, f32[4,5,8,8]{3,2,1,0:T(8,128)} %parent.1, f32[16,256,128]{2,1,0:T(8,128)} %constant.4.clone.wide_y.wide_x, ...), custom_call_target="tpu_custom_call" | custom-call | tf_op jit(solution)/shard_map/step_and_project/pallas_call | solution.py:469
  63.2 9.5 %synthesis.1 = f32[4,5,256,256]{3,2,1,0:T(8,128)} custom-call(f32[5,4,256,256]{3,2,1,0:T(8,128)} %get-tuple-element.7.stepped, f32[16,5,4,8,128]{4,3,2,1,0:T(8,128)} %bitcast.1, s32[256,256]{1,0:T(8,128)} %mask.3, f32[4,5]{1,0:T(4,128)} %nudge.1, f32[16,256,128]{2,1,0:T(8,128)} %constant.4.clone.wide_y.wide_x, f32[16,128,256]{2,1,0:T(8,128)} %constant.5.clone.tall_x.tall_y), custom_call_target="tpu_custom_call" | custom-call | tf_op jit(solution)/shard_map/synthesis/pallas_call | solution.py:518

commit v2 on v1

--- a/solution.py
+++ b/solution.py
@@ -10,7 +10,7 @@
 from jax.sharding import PartitionSpec as P
 
 MESH = pl.DeviceIdType.MESH
-STRIP = 16
+STRIP = 64
 PAD = 8
 HALO = 24
 
@@ -45,7 +45,7 @@
     fields, mask, diff, cor, parent, wide_y, tall_x,
     stepped, gap,
     q_s, m_s, mi_s, di_s, co_s, yf_s, xf_s, ey_s, ex_s, coef, out_s, hi_s, lo_s,
-    rp, rh, cp, ch, pack, hc,
+    rp, rh, cp, ch, pack, hc, fix_row,
     part, core_in, mine, chip_in, row_s, rt, y_in, pt, gt, blk,
     in_sem, tab_sem, halo_send, halo_recv, out_sem,
     core_send, core_recv, chip_send, chip_recv, y_send, y_recv, g_send, g_recv,
@@ -53,6 +53,7 @@
 ):
     n_gx, n_gy, n_f, n_l, tx, ty, modes = dims
     n_j = n_gx // 2
+    n_h = ty // 128
     kb = modes // n_gx
     kyb = modes // n_gy
     n_fl = n_f * n_l
@@ -73,9 +74,11 @@
     def to_y(i):
         return (gx, i)
 
-    def load(l):
+    def load(l, h):
         return pltpu.make_async_copy(
-            fields.at[:, l], q_s.at[l, :, pl.ds(PAD, tx), :], in_sem.at[l]
+            fields.at[:, l, :, pl.ds(h * 128, 128)],
+            q_s.at[l, :, h, pl.ds(PAD, tx), :],
+            in_sem.at[l, h],
         )
 
     small = [
@@ -88,7 +91,8 @@
     for c in small[:2]:
         c.start()
     for l in range(n_l):
-        load(l).start()
+        for h in range(n_h):
+            load(l, h).start()
     for c in small[2:]:
         c.start()
 
@@ -108,29 +112,36 @@
     lane = lax.broadcasted_iota(jnp.int32, (tx, 128), 1)
     for c in small[:2]:
         c.wait()
-    m = mi_s[...].astype(jnp.float32)
-    m_s[0, pl.ds(PAD, tx), :] = m
-    m_s[1, pl.ds(PAD, tx), :] = di_s[...] * m
+    m_s[0] = mi_s[...].astype(jnp.float32)
+    m_s[1] = di_s[...] * m_s[0]
     for side in range(2):
         rp[side, pl.ds(n_fl, HALO - n_fl), :] = jnp.zeros((HALO - n_fl, ty), jnp.float32)
-        at = PAD if side == 0 else PAD + tx - 1
+        at = 0 if side == 0 else tx - 1
         col = 0 if side == 0 else ty - 1
         acc = jnp.zeros((tx, 128), jnp.float32)
         for k in range(2):
             rp[side, n_fl + k : n_fl + k + 1, :] = m_s[k, at : at + 1, :]
-            edge = jnp.broadcast_to(m_s[k, PAD : PAD + tx, col : col + 1], (tx, 128))
+            edge = jnp.broadcast_to(m_s[k, :, col : col + 1], (tx, 128))
             acc = jnp.where(lane == n_fl + k, edge, acc)
         pack[side] = acc
 
     def pack_level(l, carry):
-        load(l).wait()
+        for h in range(n_h):
+            load(l, h).wait()
+        for f in range(n_f):
+            for h in range(n_h):
+                q_s[l, f, h, pl.ds(0, PAD), :] = jnp.zeros((PAD, 128), jnp.float32)
+                q_s[l, f, h, pl.ds(PAD + tx, PAD), :] = jnp.zeros((PAD, 128), jnp.float32)
         for side in range(2):
             at = PAD if side == 0 else PAD + tx - 1
-            col = 0 if side == 0 else ty - 1
+            h_edge, col = (0, 0) if side == 0 else (n_h - 1, 127)
             acc = pack[side]
             for f in range(n_f):
-                rp[side, pl.ds(l * n_f + f, 1), :] = q_s[l, f, at : at + 1, :]
-                edge = jnp.broadcast_to(q_s[l, f, PAD : PAD + tx, col : col + 1], (tx, 128))
+                row = [q_s[l, f, h, at : at + 1, :] for h in range(n_h)]
+                rp[side, pl.ds(l * n_f + f, 1), :] = jnp.concatenate(row, axis=1)
+                edge = jnp.broadcast_to(
+                    q_s[l, f, h_edge, PAD : PAD + tx, col : col + 1], (tx, 128)
+                )
                 acc = jnp.where(lane == l * n_f + f, edge, acc)
             pack[side] = acc
         return carry
@@ -138,6 +149,63 @@
     lax.fori_loop(0, n_l, pack_level, 0)
     for side in range(2):
         cp[side] = pack[side].T[:HALO]
+
+    for c in small[2:]:
+        c.wait()
+    row_id = lax.broadcasted_iota(jnp.int32, (tx, ty), 0)
+    col_id = lax.broadcasted_iota(jnp.int32, (tx, ty), 1)
+
+    def shifted(v):
+        return (
+            pltpu.roll(v, tx - 1, 0), pltpu.roll(v, 1, 0),
+            pltpu.roll(v, ty - 1, 1), pltpu.roll(v, 1, 1),
+        )
+
+    m, km = m_s[0], m_s[1]
+    inner = (row_id < tx - 1, row_id > 0, col_id < ty - 1, col_id > 0)
+    total = jnp.zeros((tx, ty), jnp.float32)
+    for k, (m_n, k_n) in enumerate(zip(shifted(m), shifted(km))):
+        e = jnp.where(inner[k], 0.5 * (km * m_n + m * k_n), 0.0)
+        total = total + e
+        for h in range(n_h):
+            coef[k, h] = (m * e)[:, h * 128 : (h + 1) * 128]
+    diagonal = m * (1.0 - total)
+    turn = m * co_s[...]
+    for h in range(n_h):
+        coef[4, h] = diagonal[:, h * 128 : (h + 1) * 128]
+        coef[5, h] = turn[:, h * 128 : (h + 1) * 128]
+
+    lane_s = lax.broadcasted_iota(jnp.int32, (STRIP, 128), 1)
+    is_first = lane_s == 0
+    is_last = lane_s == 127
+
+    def stencil(l, carry):
+        def strip(i, c):
+            r0 = pl.multiple_of(i * STRIP, STRIP)
+            here = pl.ds(r0, STRIP)
+            mid = pl.ds(r0 + PAD, STRIP)
+            for f in range(n_f):
+                q = [q_s[l, f, h, mid, :] for h in range(n_h)]
+                south = [pltpu.roll(v, 1, 1) for v in q]
+                north = [pltpu.roll(v, 127, 1) for v in q]
+                for h in range(n_h):
+                    s = south[h] if h == 0 else jnp.where(is_first, south[h - 1], south[h])
+                    n = north[h] if h == n_h - 1 else jnp.where(is_last, north[h + 1], north[h])
+                    w = q_s[l, f, h, pl.ds(r0 + PAD - 1, STRIP), :]
+                    e = q_s[l, f, h, pl.ds(r0 + PAD + 1, STRIP), :]
+                    value = coef[4, h, here, :] * q[h]
+                    value = value + (coef[0, h, here, :] * e + coef[1, h, here, :] * w)
+                    value = value + (coef[2, h, here, :] * n + coef[3, h, here, :] * s)
+                    if f == 2:
+                        value = value + coef[5, h, here, :] * q_s[l, 3, h, mid, :]
+                    if f == 3:
+                        value = value - coef[5, h, here, :] * q_s[l, 2, h, mid, :]
+                    out_s[l, f, here, pl.ds(h * 128, 128)] = value
+            return c
+
+        return lax.fori_loop(0, tx // STRIP, strip, carry)
+
+    lax.fori_loop(0, n_l // 2, stencil, 0)
 
     pl.semaphore_wait(barrier, 3 + (n_j - 1) + (n_gy - 1))
 
@@ -156,8 +224,6 @@
     for k in range(4):
         halo_copy(k).start()
 
-    for c in small[2:]:
-        c.wait()
     ey_s[:, :modes], ey_s[:, modes:] = split(yf_s[...])
     ex_s[:modes, :], ex_s[modes:, :] = split(xf_s[...])
     pack_rows = n_t * 128
@@ -169,6 +235,8 @@
         pt[t] = blk[t * 128 : (t + 1) * 128, :].T[:kyb]
     row_s[...] = jnp.zeros((pack_rows, 128), jnp.float32)
 
+    lax.fori_loop(n_l // 2, n_l, stencil, 0)
+
     for k in range(4):
         halo_copy(k).wait_recv()
 
@@ -179,57 +247,15 @@
         (gy < n_gy - 1).astype(jnp.float32),
     ]
     for side in range(2):
-        at = PAD - 1 if side == 0 else PAD + tx
-        for k in range(2):
-            m_s[k, at : at + 1, :] = rh[side, n_fl + k : n_fl + k + 1, :] * has[side]
-
-        def put(l, carry, side=side, at=at):
-            for f in range(n_f):
-                q_s[l, f, at : at + 1, :] = rh[side, pl.ds(l * n_f + f, 1), :]
-            return carry
-
-        lax.fori_loop(0, n_l, put, 0)
-        hc[side] = ch[side].T
-
-    lane_s = lax.broadcasted_iota(jnp.int32, (STRIP, 128), 1)
-    is_first = lane_s == 0
-    is_last = lane_s == 127
-
-    def neighbours(v, r0, slot, scale=None):
-        span = STRIP + 2 * PAD
-        q = v[PAD : PAD + STRIP]
-        west = pltpu.roll(v, 1, 0)[PAD : PAD + STRIP]
-        east = pltpu.roll(v, span - 1, 0)[PAD : PAD + STRIP]
-        h_lo = pltpu.roll(hc[0, pl.ds(r0, STRIP), :], lax.rem(128 - slot, 128), 1)
-        h_hi = pltpu.roll(hc[1, pl.ds(r0, STRIP), :], 127 - slot, 1)
-        if scale is not None:
-            h_lo, h_hi = h_lo * scale[0], h_hi * scale[1]
-        south = pltpu.roll(q, 1, 1)
-        north = pltpu.roll(q, ty - 1, 1)
-        south = jnp.concatenate(
-            [jnp.where(is_first, h_lo, south[:, :128]), south[:, 128:]], axis=1
-        )
-        north = jnp.concatenate(
-            [north[:, : ty - 128], jnp.where(is_last, h_hi, north[:, ty - 128 :])], axis=1
-        )
-        return q, east, west, north, south
-
-    def coef_strip(i, carry):
-        r0 = pl.multiple_of(i * STRIP, STRIP)
-        window = pl.ds(r0, STRIP + 2 * PAD)
-        ms = neighbours(m_s[0, window, :], r0, n_fl, (has[2], has[3]))
-        ks = neighbours(m_s[1, window, :], r0, n_fl + 1, (has[2], has[3]))
-        here = pl.ds(r0, STRIP)
-        total = None
-        for k in range(4):
-            e = 0.5 * (ks[0] * ms[1 + k] + ms[0] * ks[1 + k])
-            coef[k, here, :] = ms[0] * e
-            total = e if total is None else total + e
-        coef[4, here, :] = ms[0] * (1.0 - total)
-        coef[5, here, :] = ms[0] * co_s[here, :]
-        return carry
-
-    lax.fori_loop(0, tx // STRIP, coef_strip, 0)
+        own, far = rp[side], rh[side]
+        m_a, k_a = own[n_fl : n_fl + 1], own[n_fl + 1 : n_fl + 2]
+        m_b, k_b = far[n_fl : n_fl + 1] * has[side], far[n_fl + 1 : n_fl + 2] * has[side]
+        fix_row[side] = (m_a * (0.5 * (k_a * m_b + m_a * k_b))) * (far - own)
+        own, far = pack[side], ch[side].T
+        m_a, k_a = own[:, n_fl : n_fl + 1], own[:, n_fl + 1 : n_fl + 2]
+        m_b = far[:, n_fl : n_fl + 1] * has[2 + side]
+        k_b = far[:, n_fl + 1 : n_fl + 2] * has[2 + side]
+        hc[side] = (m_a * (0.5 * (k_a * m_b + m_a * k_b))) * (far - own)
 
     def core_copy(l):
         return pltpu.make_async_remote_copy(
@@ -263,23 +289,28 @@
         lax.fori_loop(1, n_j, lambda d, c: (chip_copy(l, d).start(), c)[1], 0)
 
     def level(l, carry):
+        for f in range(n_f):
+            slot = pl.ds(l * n_f + f, 1)
+            out_s[l, f, 0:1, :] = out_s[l, f, 0:1, :] + fix_row[0, slot, :]
+            out_s[l, f, tx - 1 : tx, :] = out_s[l, f, tx - 1 : tx, :] + fix_row[1, slot, :]
+
         def strip(i, c):
             r0 = pl.multiple_of(i * STRIP, STRIP)
             here = pl.ds(r0, STRIP)
-            window = pl.ds(r0, STRIP + 2 * PAD)
-            ce, cw, cn, cs, cc, ck = [coef[k, here, :] for k in range(6)]
-            turn = {}
             for f in range(n_f):
-                q, e, w, n, s = neighbours(q_s[l, f, window, :], r0, l * n_f + f)
-                value = cc * q + (ce * e + cw * w) + (cn * n + cs * s)
-                if f == 2:
-                    value = value + ck * q_s[l, 3, pl.ds(r0 + PAD, STRIP), :]
-                if f == 3:
-                    value = value - ck * q_s[l, 2, pl.ds(r0 + PAD, STRIP), :]
-                out_s[l, f, here, :] = value
-                hi, lo = split(value)
-                hi_s[f, here, :] = hi
-                lo_s[f, here, :] = lo
+                slot = l * n_f + f
+                low = pltpu.roll(hc[0, here, :], lax.rem(128 - slot, 128), 1)
+                top = pltpu.roll(hc[1, here, :], 127 - slot, 1)
+                for h in range(n_h):
+                    lanes = pl.ds(h * 128, 128)
+                    value = out_s[l, f, here, lanes]
+                    if h == 0:
+                        value = value + jnp.where(is_first, low, 0.0)
+                    if h == n_h - 1:
+                        value = value + jnp.where(is_last, top, 0.0)
+                    if h in (0, n_h - 1):
+                        out_s[l, f, here, lanes] = value
+                    hi_s[f, here, lanes], lo_s[f, here, lanes] = split(value)
             return c
 
         lax.fori_loop(0, tx // STRIP, strip, 0)
@@ -417,35 +448,59 @@
 
 
 def synth_kernel(
-    dims, stepped, gap, mask, nudge, wide_x, tall_y, out, xf_s, yf_s, ex_s, ey_s, m_s, sem
+    dims, stepped, gap, mask, nudge, wide_x, tall_y, out,
+    st, g_s, mi_s, xf_s, yf_s, ex_s, ey_s, m_s, sem, st_sem, out_sem,
 ):
     n_gx, n_gy, n_f, n_l, tx, ty, modes = dims
-    l = pl.program_id(0)
-
-    @pl.when(l == 0)
-    def _():
-        copies = [
-            pltpu.make_async_copy(wide_x.at[lax.axis_index("gx")], xf_s, sem.at[0]),
-            pltpu.make_async_copy(tall_y.at[lax.axis_index("gy")], yf_s, sem.at[1]),
-        ]
-        for c in copies:
-            c.start()
-        m_s[...] = mask[...].astype(jnp.float32)
-        for c in copies:
-            c.wait()
-        ex_s[:, :modes], ex_s[:, modes:] = split(xf_s[...])
-        ey_s[:modes, :], ey_s[modes:, :] = split(yf_s[...])
-
-    g = jnp.concatenate([gap[:, 0, f].reshape(modes, modes) for f in range(n_f)], axis=0)
-    g_hi, g_lo = split(g)
-    y_hi = ey_s[:modes, :]
-    right = dot(g_hi, y_hi) + dot(g_lo, y_hi) + dot(g_hi, ey_s[modes:, :])
-    r_hi, r_lo = split(right)
-    for f in range(n_f):
-        here = slice(f * modes, (f + 1) * modes)
-        twice = jnp.concatenate([r_hi[here], r_hi[here]], axis=0)
-        corr = dot(ex_s[...], twice) + dot(ex_s[:, :modes], r_lo[here])
-        out[f, 0] = stepped[0, f] + (nudge[f, l] * m_s[...]) * corr
+    kb = modes // n_gx
+    first = [
+        pltpu.make_async_copy(tall_y.at[lax.axis_index("gy")], yf_s, sem.at[0]),
+        pltpu.make_async_copy(gap, g_s, sem.at[1]),
+        pltpu.make_async_copy(wide_x.at[lax.axis_index("gx")], xf_s, sem.at[2]),
+        pltpu.make_async_copy(mask, mi_s, sem.at[3]),
+    ]
+    for c in first:
+        c.start()
+
+    def load(l):
+        return pltpu.make_async_copy(stepped.at[l], st.at[l], st_sem.at[l])
+
+    def store(l, f):
+        return pltpu.make_async_copy(st.at[l, f], out.at[f, l], out_sem.at[l, f])
+
+    for l in range(n_l):
+        load(l).start()
+    for c in first:
+        c.wait()
+    ex_s[:, :modes], ex_s[:, modes:] = split(xf_s[...])
+    ey_s[:modes, :], ey_s[modes:, :] = split(yf_s[...])
+    m_s[...] = mi_s[...].astype(jnp.float32)
+
+    def level(l, carry):
+        g = jnp.concatenate(
+            [
+                g_s[:, pl.ds((l * n_f + f) * kb, kb), :].reshape(modes, modes)
+                for f in range(n_f)
+            ],
+            axis=0,
+        )
+        g_hi, g_lo = split(g)
+        y_hi = ey_s[:modes, :]
+        right = dot(g_hi, y_hi) + dot(g_lo, y_hi) + dot(g_hi, ey_s[modes:, :])
+        r_hi, r_lo = split(right)
+        load(l).wait()
+        for f in range(n_f):
+            here = slice(f * modes, (f + 1) * modes)
+            twice = jnp.concatenate([r_hi[here], r_hi[here]], axis=0)
+            corr = dot(ex_s[...], twice) + dot(ex_s[:, :modes], r_lo[here])
+            st[l, f] = st[l, f] + (nudge[f, l] * m_s[...]) * corr
+            store(l, f).start()
+        return carry
+
+    lax.fori_loop(0, n_l, level, 0)
+    for l in range(n_l):
+        for f in range(n_f):
+            store(l, f).wait()
 
 
 def body(n_gx, n_gy, fields, sea_mask, diffusivity, coriolis, nudge_weight, parent_modes):
@@ -456,6 +511,7 @@
     rows = n_fl * kb
     n_t = -(-rows // 128)
     n_j = n_gx // 2
+    n_h = ty // 128
     dims = (n_gx, n_gy, n_f, n_l, tx, ty, modes)
     wide_x, tall_x = [jnp.asarray(t) for t in basis_pair(tx * n_gx, modes, n_gx)]
     if (tx, n_gx) == (ty, n_gy):
@@ -475,8 +531,8 @@
         in_specs=[any_space] * 4 + [vmem] + [any_space] * 2,
         out_specs=(any_space, any_space),
         scratch_shapes=[
-            pltpu.VMEM((n_l, n_f, tx + 2 * PAD, ty), f32),
-            pltpu.VMEM((2, tx + 2 * PAD, ty), f32),
+            pltpu.VMEM((n_l, n_f, n_h, tx + 2 * PAD, 128), f32),
+            pltpu.VMEM((2, tx, ty), f32),
             pltpu.VMEM((tx, ty), jnp.int32),
             pltpu.VMEM((tx, ty), f32),
             pltpu.VMEM((tx, ty), f32),
@@ -484,7 +540,7 @@
             pltpu.VMEM((modes, tx), f32),
             pltpu.VMEM((ty, 2 * modes), bf16),
             pltpu.VMEM((2 * modes, tx), bf16),
-            pltpu.VMEM((6, tx, ty), f32),
+            pltpu.VMEM((6, n_h, tx, 128), f32),
             pltpu.VMEM((n_l, n_f, tx, ty), f32),
             pltpu.VMEM((n_f, tx, ty), bf16),
             pltpu.VMEM((n_f, tx, ty), bf16),
@@ -494,6 +550,7 @@
             pltpu.VMEM((2, 128, tx), f32),
             pltpu.VMEM((2, tx, 128), f32),
             pltpu.VMEM((2, tx, 128), f32),
+            pltpu.VMEM((2, HALO, ty), f32),
             pltpu.VMEM((n_l, 2, n_j, n_f, kb, 128), f32),
             pltpu.VMEM((n_l, n_j, n_f, kb, 128), f32),
             pltpu.VMEM((n_l, n_j, n_f, kb, 128), f32),
@@ -504,7 +561,7 @@
             pltpu.VMEM((n_t, kyb, 128), f32),
             pltpu.VMEM((n_gy, n_t, kyb, 128), f32),
             pltpu.VMEM((n_t * 128, 128), f32),
-            dma((n_l,)), dma((5,)), dma((4,)), dma((4,)), dma((n_l,)),
+            dma((n_l, n_h)), dma((5,)), dma((4,)), dma((4,)), dma((n_l,)),
             dma((n_l,)), dma((n_l,)), dma((n_l, n_j)), dma((n_l, n_j)),
             dma((n_gy,)), dma((n_gy,)), dma((n_gy,)), dma((n_gy,)),
             dma((n_j,)), dma((n_j,)), dma((n_j,)), dma((n_j,)), dma,
@@ -517,28 +574,25 @@
 
     return pl.pallas_call(
         functools.partial(synth_kernel, dims),
-        grid=(n_l,),
         out_shape=jax.ShapeDtypeStruct(fields.shape, f32),
-        in_specs=[
-            pl.BlockSpec((1, n_f, tx, ty), lambda l: (l, 0, 0, 0)),
-            pl.BlockSpec((n_gx, 1, n_f, kb, 128), lambda l: (0, l, 0, 0, 0)),
-            pl.BlockSpec((tx, ty), lambda l: (0, 0)),
-            pl.BlockSpec(memory_space=pltpu.SMEM),
-            any_space,
-            any_space,
-        ],
-        out_specs=pl.BlockSpec((n_f, 1, tx, ty), lambda l: (0, l, 0, 0)),
+        in_specs=[any_space] * 3 + [pl.BlockSpec(memory_space=pltpu.SMEM)] + [any_space] * 2,
+        out_specs=any_space,
         scratch_shapes=[
+            pltpu.VMEM((n_l, n_f, tx, ty), f32),
+            pltpu.VMEM((n_gx, rows, 128), f32),
+            pltpu.VMEM((tx, ty), jnp.int32),
             pltpu.VMEM((tx, modes), f32),
             pltpu.VMEM((modes, ty), f32),
             pltpu.VMEM((tx, 2 * modes), bf16),
             pltpu.VMEM((2 * modes, ty), bf16),
             pltpu.VMEM((tx, ty), f32),
-            dma((2,)),
+            dma((4,)),
+            dma((n_l,)),
+            dma((n_l, n_f)),
         ],
         compiler_params=pltpu.CompilerParams(vmem_limit_bytes=60 * 2**20),
         name="synthesis",
-    )(stepped, gap.reshape(n_gx, n_l, n_f, kb, 128), sea_mask, nudge_weight, wide_x, tall_y)
+    )(stepped, gap, sea_mask, nudge_weight, wide_x, tall_y)
 
 
 def solution(mesh):

time: 73 us -> 65.8 us (0.901)
  Pallas kernels: 72.7 us -> 65.6 us
    pallas_call x1, Pallas kernels: 63.2 us -> 56 us  [body(): pl.pallas_call(functools.partial(step_kernel, dims), out_shape=(jax.Shape...]
where the time goes in v2:
time: 65.8 us; the launch traced here: 65.6 us
  Pallas kernels  65.6 us (100%)
    pallas_call x1, Pallas kernels, body(): pl.pallas_call(functools.partial(step_kernel, dims), out_shape=(jax.Shape...  56 us
    pallas_call x1, Pallas kernels, body(): pl.pallas_call(functools.partial(synth_kernel, dims), out_shape=jax.Shape...  9.64 us

profile of v2, /device:TPU:1, one launch (start us, length us, event | category | flops | bytes accessed | tf_op | source)
XLA Modules:
  0.0 65.6 jit_solution(14818733477083992516)
XLA Ops:
  0.0 56.0 %step_and_project.1 = (f32[5,4,256,256]{3,2,1,0:T(8,128)}, f32[16,160,128]{2,1,0:T(8,128)}) custom-call(f32[4,5,256,256]{3,2,1,0:T(8,128)} %fields.1, s32[256,256]{1,0:T(8,128)} %mask.3, f32[256,256]{1,0:T(8,128)} %diff.1, f32[256,256]{1,0:T(8,128)} %cor.1, f32[4,5,8,8]{3,2,1,0:T(8,128)} %parent.1, f32[16,256,128]{2,1,0:T(8,128)} %constant.4.clone.wide_y.wide_x, ...), custom_call_target="tpu_custom_call" | custom-call | tf_op jit(solution)/shard_map/step_and_project/pallas_call | solution.py:525
  56.0 9.6 %synthesis.1 = f32[4,5,256,256]{3,2,1,0:T(8,128)} custom-call(f32[5,4,256,256]{3,2,1,0:T(8,128)} %get-tuple-element.7.stepped, f32[16,160,128]{2,1,0:T(8,128)} %get-tuple-element.8.gap, s32[256,256]{1,0:T(8,128)} %mask.3, f32[4,5]{1,0:T(4,128)} %nudge.1, f32[16,256,128]{2,1,0:T(8,128)} %constant.4.clone.wide_y.wide_x, ...), custom_call_target="tpu_custom_call" | custom-call | tf_op jit(solution)/shard_map/synthesis/pallas_call | solution.py:575

commit v3 on v2

--- a/solution.py
+++ b/solution.py
@@ -30,6 +30,11 @@
     return wide, np.ascontiguousarray(np.swapaxes(wide, 1, 2))
 
 
+def chunk_levels(n_l):
+    step = 2 if n_l > 2 else 1
+    return [(l, min(step, n_l - l)) for l in range(0, n_l, step)]
+
+
 def split(value):
     high = value.astype(jnp.bfloat16)
     low = (value - high.astype(jnp.float32)).astype(jnp.bfloat16)
@@ -42,14 +47,15 @@
 
 def step_kernel(
     dims,
-    fields, mask, diff, cor, parent, wide_y, tall_x,
-    stepped, gap,
-    q_s, m_s, mi_s, di_s, co_s, yf_s, xf_s, ey_s, ex_s, coef, out_s, hi_s, lo_s,
+    fields, mask, diff, cor, parent_in, wide_y, tall_x, wide_x, tall_y,
+    stepped, gap, sea, wide_out, tall_out,
+    parent, q_s, m_s, mi_s, di_s, co_s, yf_s, xf_s, wf_s, tf_s, ey_s, ex_s, wo_s, to_s,
+    coef, out_s, hi_s, lo_s,
     rp, rh, cp, ch, pack, hc, fix_row,
-    part, core_in, mine, chip_in, row_s, rt, y_in, pt, gt, blk,
+    part, core_in, mine, chip_in, row_s, rt, z_in, pth, pt, gt, blk,
     in_sem, tab_sem, halo_send, halo_recv, out_sem,
-    core_send, core_recv, chip_send, chip_recv, y_send, y_recv, g_send, g_recv,
-    b_send, b_recv, f_send, f_recv, own_sem,
+    core_send, core_recv, chip_send, chip_recv, z_send, z_recv, g_send, g_recv,
+    b_send, b_recv, f_send, f_recv, p_sem, own_sem,
 ):
     n_gx, n_gy, n_f, n_l, tx, ty, modes = dims
     n_j = n_gx // 2
@@ -57,14 +63,21 @@
     kb = modes // n_gx
     kyb = modes // n_gy
     n_fl = n_f * n_l
-    rows = n_fl * kb
+    n_fh = n_f // 2
+    n_z = n_gy // 2
+    n_p = 2 * n_j
+    kz = 2 * kyb
+    rows = n_l * n_fh * kb
     n_t = rt.shape[1]
+    chunks = chunk_levels(n_l)
     gx = lax.axis_index("gx")
     gy = lax.axis_index("gy")
     core = lax.rem(gx, 2)
     chip = lax.div(gx, 2)
     other = 1 - core
     partner = 2 * chip + other
+    z, y_lo = lax.div(gy, 2), lax.rem(gy, 2)
+    plane = 2 * chip + y_lo
     up_x, dn_x = lax.rem(gx + 1, n_gx), lax.rem(gx + n_gx - 1, n_gx)
     up_y, dn_y = lax.rem(gy + 1, n_gy), lax.rem(gy + n_gy - 1, n_gy)
 
@@ -73,6 +86,14 @@
 
     def to_y(i):
         return (gx, i)
+
+    def to_plane(q):
+        return (2 * lax.div(q, 2) + core, 2 * z + lax.rem(q, 2))
+
+    def to_z(i):
+        return (gx, 2 * i + y_lo)
+
+    side_y = to_y(2 * z + 1 - y_lo)
 
     def load(l, h):
         return pltpu.make_async_copy(
@@ -87,6 +108,9 @@
         pltpu.make_async_copy(cor, co_s, tab_sem.at[2]),
         pltpu.make_async_copy(wide_y.at[gy], yf_s, tab_sem.at[3]),
         pltpu.make_async_copy(tall_x.at[gx], xf_s, tab_sem.at[4]),
+        pltpu.make_async_copy(wide_x.at[gx], wf_s, tab_sem.at[5]),
+        pltpu.make_async_copy(tall_y.at[gy], tf_s, tab_sem.at[6]),
+        pltpu.make_async_copy(parent_in, parent, tab_sem.at[7]),
     ]
     for c in small[:2]:
         c.start()
@@ -106,8 +130,11 @@
     greet(to_x(up_x))
     greet(to_x(dn_x))
     greet(to_x(partner))
-    lax.fori_loop(1, n_j, lambda d, c: (greet(to_x(2 * lax.rem(chip + d, n_j) + core)), c)[1], 0)
-    lax.fori_loop(1, n_gy, lambda d, c: (greet(to_y(lax.rem(gy + d, n_gy))), c)[1], 0)
+    greet(to_y(up_y))
+    greet(to_y(dn_y))
+    greet(side_y)
+    lax.fori_loop(1, n_p, lambda d, c: (greet(to_plane(lax.rem(plane + d, n_p))), c)[1], 0)
+    lax.fori_loop(1, n_z, lambda d, c: (greet(to_z(lax.rem(z + d, n_z))), c)[1], 0)
 
     lane = lax.broadcasted_iota(jnp.int32, (tx, 128), 1)
     for c in small[:2]:
@@ -207,7 +234,7 @@
 
     lax.fori_loop(0, n_l // 2, stencil, 0)
 
-    pl.semaphore_wait(barrier, 3 + (n_j - 1) + (n_gy - 1))
+    pl.semaphore_wait(barrier, 6 + (n_p - 1) + (n_z - 1))
 
     def halo_copy(k):
         src, dst, dev = [
@@ -227,13 +254,33 @@
     ey_s[:, :modes], ey_s[:, modes:] = split(yf_s[...])
     ex_s[:modes, :], ex_s[modes:, :] = split(xf_s[...])
     pack_rows = n_t * 128
-    blk[...] = jnp.zeros((pack_rows, 128), jnp.float32)
-    for f in range(n_f):
-        for l in range(n_l):
-            blk[pl.ds((l * n_f + f) * kb, kb), pl.ds(0, kyb)] = parent[f, l]
-    for t in range(n_t):
-        pt[t] = blk[t * 128 : (t + 1) * 128, :].T[:kyb]
+    for half in range(2):
+        blk[...] = jnp.zeros((pack_rows, 128), jnp.float32)
+        for f in range(n_fh):
+            for l in range(n_l):
+                blk[pl.ds((l * n_fh + f) * kb, kb), pl.ds(0, kyb)] = parent[half * n_fh + f, l]
+        for t in range(n_t):
+            pth[half, t] = blk[t * 128 : (t + 1) * 128, :].T[:kyb]
+    parent_copy = pltpu.make_async_remote_copy(
+        src_ref=pth.at[1 - y_lo], dst_ref=pt.at[y_lo],
+        send_sem=p_sem.at[0], recv_sem=p_sem.at[1],
+        device_id=side_y, device_id_type=MESH,
+    )
+    parent_copy.start()
+    pt[y_lo] = pth[y_lo]
     row_s[...] = jnp.zeros((pack_rows, 128), jnp.float32)
+    wo_s[:, :modes], wo_s[:, modes:] = split(wf_s[...])
+    t_hi, t_lo = split(tf_s[...])
+    to_s[:modes, :] = t_hi
+    to_s[modes : 2 * modes, :] = t_hi
+    to_s[2 * modes :, :] = t_lo
+    given = [
+        pltpu.make_async_copy(m_s.at[0], sea, own_sem.at[1]),
+        pltpu.make_async_copy(wo_s, wide_out, own_sem.at[2]),
+        pltpu.make_async_copy(to_s, tall_out, own_sem.at[3]),
+    ]
+    for c in given:
+        c.start()
 
     lax.fori_loop(n_l // 2, n_l, stencil, 0)
 
@@ -264,29 +311,25 @@
             device_id=to_x(partner), device_id_type=MESH,
         )
 
-    def chip_copy(l, d):
-        there = lax.rem(chip + d, n_j)
+    def chip_copy(k, d, arrival=False):
+        l0, span = chunks[k]
+        there = lax.rem(plane + d, n_p)
+        slot = there if arrival else plane
         return pltpu.make_async_remote_copy(
-            src_ref=mine.at[l, there], dst_ref=chip_in.at[l, chip],
-            send_sem=chip_send.at[l, there], recv_sem=chip_recv.at[l, chip],
-            device_id=to_x(2 * there + core), device_id_type=MESH,
-        )
-
-    def chip_arrival(l, d):
-        there = lax.rem(chip + d, n_j)
-        return pltpu.make_async_remote_copy(
-            src_ref=mine.at[l, there], dst_ref=chip_in.at[l, there],
-            send_sem=chip_send.at[l, there], recv_sem=chip_recv.at[l, there],
-            device_id=to_x(2 * there + core), device_id_type=MESH,
+            src_ref=mine.at[pl.ds(l0, span), there], dst_ref=chip_in.at[pl.ds(l0, span), slot],
+            send_sem=chip_send.at[k, there], recv_sem=chip_recv.at[k, slot],
+            device_id=to_plane(there), device_id_type=MESH,
         )
 
     def out_copy(l):
         return pltpu.make_async_copy(out_s.at[l], stepped.at[l], out_sem.at[l])
 
-    def pass_on(l):
-        core_copy(l).wait_recv()
-        mine[l] = part[l, core] + core_in[l]
-        lax.fori_loop(1, n_j, lambda d, c: (chip_copy(l, d).start(), c)[1], 0)
+    def pass_on(k):
+        l0, span = chunks[k]
+        for l in range(l0, l0 + span):
+            core_copy(l).wait_recv()
+            mine[l] = part[l, core] + core_in[l]
+        lax.fori_loop(1, n_p, lambda d, c: (chip_copy(k, d).start(), c)[1], 0)
 
     def level(l, carry):
         for f in range(n_f):
@@ -327,173 +370,155 @@
         proj = both[:modes] + both[modes:] + dot(ex_s[:modes, :], beside(left_lo))
         for g in range(n_gx):
             for f in range(n_f):
-                part[l, g % 2, g // 2, f] = proj[
+                part[l, g % 2, 2 * (g // 2) + f // n_fh, f % n_fh] = proj[
                     g * kb : (g + 1) * kb, f * modes : (f + 1) * modes
                 ]
         core_copy(l).start()
 
-        @pl.when(l > 0)
-        def _():
-            pass_on(l - 1)
+        for k in range(len(chunks) - 1):
+            pl.when(l == sum(chunks[k]))(functools.partial(pass_on, k))
 
         return carry
 
     lax.fori_loop(0, n_l, level, 0)
-    pass_on(n_l - 1)
-
-    def sum_level(l, carry):
-        total = mine[l, chip]
-
-        def add(d, t):
-            chip_arrival(l, d).wait_recv()
-            return t + chip_in[l, lax.rem(chip + d, n_j)]
-
-        total = lax.fori_loop(1, n_j, add, total)
-        row_s[pl.ds(pl.multiple_of(l * n_f * kb, 8), n_f * kb), :] = total.reshape(n_f * kb, 128)
-        return carry
-
-    lax.fori_loop(0, n_l, sum_level, 0)
+    pass_on(len(chunks) - 1)
+
+    for k, (l0, span) in enumerate(chunks):
+
+        def add(d, t, k=k, l0=l0, span=span):
+            chip_copy(k, d, True).wait_recv()
+            return t + chip_in[l0 : l0 + span, lax.rem(plane + d, n_p)]
+
+        total = lax.fori_loop(1, n_p, add, mine[l0 : l0 + span, plane])
+        row_s[l0 * n_fh * kb : (l0 + span) * n_fh * kb, :] = total.reshape(span * n_fh * kb, 128)
     for t in range(n_t):
-        rt[:, t] = row_s[t * 128 : (t + 1) * 128, :].T.reshape(n_gy, kyb, 128)
-
-    def y_copy(d, arrival=False):
-        there = lax.rem(gy + d, n_gy)
-        slot = there if arrival else gy
+        rt[:, t] = row_s[t * 128 : (t + 1) * 128, :].T.reshape(n_z, kz, 128)
+
+    def z_copy(d, arrival=False):
+        there = lax.rem(z + d, n_z)
+        slot = there if arrival else z
         return pltpu.make_async_remote_copy(
-            src_ref=rt.at[there], dst_ref=y_in.at[slot],
-            send_sem=y_send.at[there], recv_sem=y_recv.at[slot],
-            device_id=to_y(there), device_id_type=MESH,
-        )
-
-    lax.fori_loop(1, n_gy, lambda d, c: (y_copy(d).start(), c)[1], 0)
-
-    def y_add(d, t):
-        y_copy(d, True).wait_recv()
-        return t + y_in[lax.rem(gy + d, n_gy)]
-
-    total = lax.fori_loop(1, n_gy, y_add, rt[gy])
-    gt[gy] = pt[...] - total
+            src_ref=rt.at[there], dst_ref=z_in.at[slot],
+            send_sem=z_send.at[there], recv_sem=z_recv.at[slot],
+            device_id=to_z(there), device_id_type=MESH,
+        )
+
+    lax.fori_loop(1, n_z, lambda d, c: (z_copy(d).start(), c)[1], 0)
+    parent_copy.wait_recv()
+    target = jnp.concatenate([pt[0], pt[1]], axis=1)
+
+    def z_add(d, t):
+        z_copy(d, True).wait_recv()
+        return t + z_in[lax.rem(z + d, n_z)]
+
+    total = lax.fori_loop(1, n_z, z_add, rt[z])
+    gt[z] = target - total
 
     def g_copy(d, arrival=False):
-        there = lax.rem(gy + d, n_gy)
-        slot = there if arrival else gy
+        there = lax.rem(z + d, n_z)
+        slot = there if arrival else z
         return pltpu.make_async_remote_copy(
-            src_ref=gt.at[gy], dst_ref=gt.at[slot],
+            src_ref=gt.at[z], dst_ref=gt.at[slot],
             send_sem=g_send.at[there], recv_sem=g_recv.at[slot],
-            device_id=to_y(there), device_id_type=MESH,
-        )
-
-    lax.fori_loop(1, n_gy, lambda d, c: (g_copy(d).start(), c)[1], 0)
-    lax.fori_loop(1, n_gy, lambda d, c: (g_copy(d, True).wait_recv(), c)[1], 0)
+            device_id=to_z(there), device_id_type=MESH,
+        )
+
+    lax.fori_loop(1, n_z, lambda d, c: (g_copy(d).start(), c)[1], 0)
+    lax.fori_loop(1, n_z, lambda d, c: (g_copy(d, True).wait_recv(), c)[1], 0)
     for t in range(n_t):
         blk[t * 128 : (t + 1) * 128, :] = gt[:, t].reshape(128, 128).T
 
     block = blk.at[pl.ds(0, rows), :]
 
+    def place(q, c):
+        return gap.at[2 * lax.div(q, 2) + c, lax.rem(q, 2)]
+
     def b_copy(d, arrival=False):
-        there = lax.rem(chip + d, n_j)
-        slot = there if arrival else chip
+        there = lax.rem(plane + d, n_p)
+        slot = there if arrival else plane
         return pltpu.make_async_remote_copy(
-            src_ref=block, dst_ref=gap.at[2 * slot + core],
+            src_ref=block, dst_ref=place(slot, core),
             send_sem=b_send.at[there], recv_sem=b_recv.at[slot],
-            device_id=to_x(2 * there + core), device_id_type=MESH,
-        )
-
-    def f_copy(j, src=None, arrival=False):
-        at = gap.at[2 * j + (other if arrival else core)]
+            device_id=to_plane(there), device_id_type=MESH,
+        )
+
+    def f_copy(q, src=None, arrival=False):
+        at = place(q, other if arrival else core)
         return pltpu.make_async_remote_copy(
             src_ref=at if src is None else src, dst_ref=at,
-            send_sem=f_send.at[j], recv_sem=f_recv.at[j],
+            send_sem=f_send.at[q], recv_sem=f_recv.at[q],
             device_id=to_x(partner), device_id_type=MESH,
         )
 
-    lax.fori_loop(1, n_j, lambda d, c: (b_copy(d).start(), c)[1], 0)
-    f_copy(chip, block).start()
-    own = pltpu.make_async_copy(block, gap.at[gx], own_sem)
+    lax.fori_loop(1, n_p, lambda d, c: (b_copy(d).start(), c)[1], 0)
+    f_copy(plane, block).start()
+    own = pltpu.make_async_copy(block, place(plane, core), own_sem.at[0])
     own.start()
 
     def forward(d, c):
         b_copy(d, True).wait_recv()
-        f_copy(lax.rem(chip + d, n_j)).start()
+        f_copy(lax.rem(plane + d, n_p)).start()
         return c
 
-    lax.fori_loop(1, n_j, forward, 0)
-    lax.fori_loop(0, n_j, lambda j, c: (f_copy(j, None, True).wait_recv(), c)[1], 0)
+    lax.fori_loop(1, n_p, forward, 0)
+    lax.fori_loop(0, n_p, lambda q, c: (f_copy(q, None, True).wait_recv(), c)[1], 0)
 
     own.wait()
+    for c in given:
+        c.wait()
+    parent_copy.wait_send()
     for k in range(4):
         halo_copy(k).wait_send()
 
     def drain(l, c):
         out_copy(l).wait()
         core_copy(l).wait_send()
-        return lax.fori_loop(1, n_j, lambda d, e: (chip_copy(l, d).wait_send(), e)[1], c)
+        return c
 
     lax.fori_loop(0, n_l, drain, 0)
 
-    def drain_y(d, c):
-        y_copy(d).wait_send()
+    def drain_plane(d, c):
+        for k in range(len(chunks)):
+            chip_copy(k, d).wait_send()
+        b_copy(d).wait_send()
+        f_copy(lax.rem(plane + d, n_p)).wait_send()
+        return c
+
+    lax.fori_loop(1, n_p, drain_plane, 0)
+    f_copy(plane, block).wait_send()
+
+    def drain_z(d, c):
+        z_copy(d).wait_send()
         g_copy(d).wait_send()
         return c
 
-    lax.fori_loop(1, n_gy, drain_y, 0)
-
-    def drain_x(d, c):
-        b_copy(d).wait_send()
-        f_copy(lax.rem(chip + d, n_j)).wait_send()
-        return c
-
-    lax.fori_loop(1, n_j, drain_x, 0)
-    f_copy(chip, block).wait_send()
-
-
-def synth_kernel(
-    dims, stepped, gap, mask, nudge, wide_x, tall_y, out,
-    st, g_s, mi_s, xf_s, yf_s, ex_s, ey_s, m_s, sem, st_sem, out_sem,
-):
+    lax.fori_loop(1, n_z, drain_z, 0)
+
+
+def synth_kernel(dims, stepped, gap, sea, wide_x, tall_y, nudge, out, st, out_sem):
     n_gx, n_gy, n_f, n_l, tx, ty, modes = dims
     kb = modes // n_gx
-    first = [
-        pltpu.make_async_copy(tall_y.at[lax.axis_index("gy")], yf_s, sem.at[0]),
-        pltpu.make_async_copy(gap, g_s, sem.at[1]),
-        pltpu.make_async_copy(wide_x.at[lax.axis_index("gx")], xf_s, sem.at[2]),
-        pltpu.make_async_copy(mask, mi_s, sem.at[3]),
-    ]
-    for c in first:
-        c.start()
-
-    def load(l):
-        return pltpu.make_async_copy(stepped.at[l], st.at[l], st_sem.at[l])
+    n_fh = n_f // 2
 
     def store(l, f):
         return pltpu.make_async_copy(st.at[l, f], out.at[f, l], out_sem.at[l, f])
-
-    for l in range(n_l):
-        load(l).start()
-    for c in first:
-        c.wait()
-    ex_s[:, :modes], ex_s[:, modes:] = split(xf_s[...])
-    ey_s[:modes, :], ey_s[modes:, :] = split(yf_s[...])
-    m_s[...] = mi_s[...].astype(jnp.float32)
 
     def level(l, carry):
         g = jnp.concatenate(
             [
-                g_s[:, pl.ds((l * n_f + f) * kb, kb), :].reshape(modes, modes)
+                gap[:, f // n_fh, pl.ds((l * n_fh + f % n_fh) * kb, kb), :].reshape(modes, modes)
                 for f in range(n_f)
             ],
-            axis=0,
+            axis=1,
         )
         g_hi, g_lo = split(g)
-        y_hi = ey_s[:modes, :]
-        right = dot(g_hi, y_hi) + dot(g_lo, y_hi) + dot(g_hi, ey_s[modes:, :])
-        r_hi, r_lo = split(right)
-        load(l).wait()
+        t = dot(wide_x[...], jnp.concatenate([g_hi, g_hi], axis=0))
+        t_hi, t_lo = split(t + dot(wide_x[:, :modes], g_lo))
         for f in range(n_f):
             here = slice(f * modes, (f + 1) * modes)
-            twice = jnp.concatenate([r_hi[here], r_hi[here]], axis=0)
-            corr = dot(ex_s[...], twice) + dot(ex_s[:, :modes], r_lo[here])
-            st[l, f] = st[l, f] + (nudge[f, l] * m_s[...]) * corr
+            both = jnp.concatenate([t_hi[:, here], t_lo[:, here]], axis=1)
+            corr = dot(both, tall_y[: 2 * modes, :]) + dot(t_hi[:, here], tall_y[2 * modes :, :])
+            st[l, f] = stepped[l, f] + (nudge[f, l] * sea[...]) * corr
             store(l, f).start()
         return carry
 
@@ -507,9 +532,11 @@
     n_f, n_l, tx, ty = fields.shape
     modes = parent_modes.shape[2] * n_gx
     kb, kyb = modes // n_gx, modes // n_gy
-    n_fl = n_f * n_l
-    rows = n_fl * kb
+    n_fh = n_f // 2
+    rows = n_l * n_fh * kb
     n_t = -(-rows // 128)
+    n_z, n_p, kz = n_gy // 2, n_gx, 2 * kyb
+    n_k = len(chunk_levels(n_l))
     n_j = n_gx // 2
     n_h = ty // 128
     dims = (n_gx, n_gy, n_f, n_l, tx, ty, modes)
@@ -522,15 +549,21 @@
     vmem = pl.BlockSpec(memory_space=pltpu.VMEM)
     f32, bf16 = jnp.float32, jnp.bfloat16
     dma = pltpu.SemaphoreType.DMA
-    stepped, gap = pl.pallas_call(
+    hbm = functools.partial(pltpu.with_memory_space_constraint, memory_space=pltpu.HBM)
+    tables = [hbm(t) for t in (wide_y, tall_x, wide_x, tall_y)]
+    kept = pl.pallas_call(
         functools.partial(step_kernel, dims),
         out_shape=(
-            jax.ShapeDtypeStruct((n_l, n_f, tx, ty), f32),
-            jax.ShapeDtypeStruct((n_gx, rows, 128), f32),
+            pltpu.VMEM((n_l, n_f, tx, ty), f32),
+            pltpu.VMEM((n_gx, 2, rows, 128), f32),
+            pltpu.VMEM((tx, ty), f32),
+            pltpu.VMEM((tx, 2 * modes), bf16),
+            pltpu.VMEM((3 * modes, ty), bf16),
         ),
-        in_specs=[any_space] * 4 + [vmem] + [any_space] * 2,
-        out_specs=(any_space, any_space),
+        in_specs=[any_space] * 9,
+        out_specs=(any_space,) * 5,
         scratch_shapes=[
+            pltpu.VMEM(parent_modes.shape, f32),
             pltpu.VMEM((n_l, n_f, n_h, tx + 2 * PAD, 128), f32),
             pltpu.VMEM((2, tx, ty), f32),
             pltpu.VMEM((tx, ty), jnp.int32),
@@ -538,8 +571,12 @@
             pltpu.VMEM((tx, ty), f32),
             pltpu.VMEM((ty, modes), f32),
             pltpu.VMEM((modes, tx), f32),
+            pltpu.VMEM((tx, modes), f32),
+            pltpu.VMEM((modes, ty), f32),
             pltpu.VMEM((ty, 2 * modes), bf16),
             pltpu.VMEM((2 * modes, tx), bf16),
+            pltpu.VMEM((tx, 2 * modes), bf16),
+            pltpu.VMEM((3 * modes, ty), bf16),
             pltpu.VMEM((6, n_h, tx, 128), f32),
             pltpu.VMEM((n_l, n_f, tx, ty), f32),
             pltpu.VMEM((n_f, tx, ty), bf16),
@@ -551,48 +588,37 @@
             pltpu.VMEM((2, tx, 128), f32),
             pltpu.VMEM((2, tx, 128), f32),
             pltpu.VMEM((2, HALO, ty), f32),
-            pltpu.VMEM((n_l, 2, n_j, n_f, kb, 128), f32),
-            pltpu.VMEM((n_l, n_j, n_f, kb, 128), f32),
-            pltpu.VMEM((n_l, n_j, n_f, kb, 128), f32),
-            pltpu.VMEM((n_l, n_j, n_f, kb, 128), f32),
+            pltpu.VMEM((n_l, 2, n_p, n_fh, kb, 128), f32),
+            pltpu.VMEM((n_l, n_p, n_fh, kb, 128), f32),
+            pltpu.VMEM((n_l, n_p, n_fh, kb, 128), f32),
+            pltpu.VMEM((n_l, n_p, n_fh, kb, 128), f32),
             pltpu.VMEM((n_t * 128, 128), f32),
-            pltpu.VMEM((n_gy, n_t, kyb, 128), f32),
-            pltpu.VMEM((n_gy, n_t, kyb, 128), f32),
-            pltpu.VMEM((n_t, kyb, 128), f32),
-            pltpu.VMEM((n_gy, n_t, kyb, 128), f32),
+            pltpu.VMEM((n_z, n_t, kz, 128), f32),
+            pltpu.VMEM((n_z, n_t, kz, 128), f32),
+            pltpu.VMEM((2, n_t, kyb, 128), f32),
+            pltpu.VMEM((2, n_t, kyb, 128), f32),
+            pltpu.VMEM((n_z, n_t, kz, 128), f32),
             pltpu.VMEM((n_t * 128, 128), f32),
-            dma((n_l, n_h)), dma((5,)), dma((4,)), dma((4,)), dma((n_l,)),
-            dma((n_l,)), dma((n_l,)), dma((n_l, n_j)), dma((n_l, n_j)),
-            dma((n_gy,)), dma((n_gy,)), dma((n_gy,)), dma((n_gy,)),
-            dma((n_j,)), dma((n_j,)), dma((n_j,)), dma((n_j,)), dma,
+            dma((n_l, n_h)), dma((8,)), dma((4,)), dma((4,)), dma((n_l,)),
+            dma((n_l,)), dma((n_l,)), dma((n_k, n_p)), dma((n_k, n_p)),
+            dma((n_z,)), dma((n_z,)), dma((n_z,)), dma((n_z,)),
+            dma((n_p,)), dma((n_p,)), dma((n_p,)), dma((n_p,)), dma((2,)), dma((4,)),
         ],
         compiler_params=pltpu.CompilerParams(
-            collective_id=0, has_side_effects=True, vmem_limit_bytes=60 * 2**20
+            collective_id=0, has_side_effects=True, vmem_limit_bytes=46 * 2**20
         ),
         name="step_and_project",
-    )(fields, sea_mask, diffusivity, coriolis, parent_modes, wide_y, tall_x)
+    )(hbm(fields), hbm(sea_mask), hbm(diffusivity), hbm(coriolis), hbm(parent_modes), *tables)
 
     return pl.pallas_call(
         functools.partial(synth_kernel, dims),
         out_shape=jax.ShapeDtypeStruct(fields.shape, f32),
-        in_specs=[any_space] * 3 + [pl.BlockSpec(memory_space=pltpu.SMEM)] + [any_space] * 2,
+        in_specs=[vmem] * 5 + [pl.BlockSpec(memory_space=pltpu.SMEM)],
         out_specs=any_space,
-        scratch_shapes=[
-            pltpu.VMEM((n_l, n_f, tx, ty), f32),
-            pltpu.VMEM((n_gx, rows, 128), f32),
-            pltpu.VMEM((tx, ty), jnp.int32),
-            pltpu.VMEM((tx, modes), f32),
-            pltpu.VMEM((modes, ty), f32),
-            pltpu.VMEM((tx, 2 * modes), bf16),
-            pltpu.VMEM((2 * modes, ty), bf16),
-            pltpu.VMEM((tx, ty), f32),
-            dma((4,)),
-            dma((n_l,)),
-            dma((n_l, n_f)),
-        ],
-        compiler_params=pltpu.CompilerParams(vmem_limit_bytes=60 * 2**20),
+        scratch_shapes=[pltpu.VMEM((n_l, n_f, tx, ty), f32), dma((n_l, n_f))],
+        compiler_params=pltpu.CompilerParams(vmem_limit_bytes=20 * 2**20),
         name="synthesis",
-    )(stepped, gap, sea_mask, nudge_weight, wide_x, tall_y)
+    )(*kept, nudge_weight)
 
 
 def solution(mesh):

time: 65.8 us -> 59.2 us (0.90)
  Pallas kernels: 65.6 us -> 59.1 us
    pallas_call x1, Pallas kernels: 9.64 us -> 5 us  [body(): pl.pallas_call(functools.partial(synth_kernel, dims), out_shape=jax.Shape...]
    pallas_call x1, Pallas kernels: 56 us -> 54.1 us  [body(): pl.pallas_call(functools.partial(step_kernel, dims), out_shape=(pltpu.VME...]
where the time goes in v3:
time: 59.2 us; the launch traced here: 59.1 us
  Pallas kernels  59.1 us (100%)
    pallas_call x1, Pallas kernels, body(): pl.pallas_call(functools.partial(step_kernel, dims), out_shape=(pltpu.VME...  54.1 us
    pallas_call x1, Pallas kernels, body(): pl.pallas_call(functools.partial(synth_kernel, dims), out_shape=jax.Shape...  5 us

profile of v3, /device:TPU:1, one launch (start us, length us, event | category | flops | bytes accessed | tf_op | source)
XLA Modules:
  0.0 59.1 jit_solution(7434254062845927575)
XLA Ops:
  0.0 0.0 copy-start
  0.0 54.1 %step_and_project.1 = (f32[5,4,256,256]{3,2,1,0:T(8,128)S(1)}, f32[16,2,80,128]{3,2,1,0:T(8,128)S(1)}, f32[256,256]{1,0:T(8,128)S(1)}, bf16[256,256]{1,0:T(8,128)(2,1)S(1)}, bf16[384,256]{1,0:T(8,128)(2,1)S(1)}) custom-call(f32[4,5,256,256]{3,2,1,0:T(8,128)} %fields.1, s32[256,256]{1,0:T(8,128)} %mask.1, f32[256,256]{1,0:T(8,128)} %diff.1, f32[256,256]{1,0:T(8,128)} %cor.1, ...), custom_call_target="tpu_custom_call" | custom-call | tf_op jit(solution)/shard_map/step_and_project/pallas_call | solution.py:554
  54.1 0.0 copy-done
  54.1 5.0 %synthesis.1 = f32[4,5,256,256]{3,2,1,0:T(8,128)} custom-call(f32[5,4,256,256]{3,2,1,0:T(8,128)S(1)} %get-tuple-element.10.stepped, f32[16,2,80,128]{3,2,1,0:T(8,128)S(1)} %get-tuple-element.11.gap, f32[256,256]{1,0:T(8,128)S(1)} %get-tuple-element.12.sea, bf16[256,256]{1,0:T(8,128)(2,1)S(1)} %get-tuple-element.13.wide_x, ...), custom_call_target="tpu_custom_call" | custom-call | tf_op jit(solution)/shard_map/synthesis/pallas_call | solution.py:613
Async XLA Ops:
  0.0 54.1 %copy-start = (f32[4,5]{1,0:T(4,128)S(1)}, f32[4,5]{1,0:T(4,128)}, u32[]{:S(2)}) copy-start(f32[4,5]{1,0:T(4,128)} %nudge.1) | copy-start | bytes 244

commit v4 on v3

--- a/solution.py
+++ b/solution.py
@@ -30,9 +30,12 @@
     return wide, np.ascontiguousarray(np.swapaxes(wide, 1, 2))
 
 
-def chunk_levels(n_l):
-    step = 2 if n_l > 2 else 1
-    return [(l, min(step, n_l - l)) for l in range(0, n_l, step)]
+def offsets(n_p, n_z):
+    n_x, n_y = n_p // 4, 4
+    plane = [(i, j) for i in range(n_x) for j in range(n_y) if i or j]
+    plane.sort(key=lambda o: -(min(o[0], n_x - o[0]) + min(o[1], n_y - o[1])))
+    line = sorted(range(1, n_z), key=lambda d: -min(d, n_z - d))
+    return plane, line
 
 
 def split(value):
@@ -54,8 +57,8 @@
     rp, rh, cp, ch, pack, hc, fix_row,
     part, core_in, mine, chip_in, row_s, rt, z_in, pth, pt, gt, blk,
     in_sem, tab_sem, halo_send, halo_recv, out_sem,
-    core_send, core_recv, chip_send, chip_recv, z_send, z_recv, g_send, g_recv,
-    b_send, b_recv, f_send, f_recv, p_sem, own_sem,
+    core_send, core_recv, chip_send, chip_recv, z_sem,
+    b_send, b_recv, f_sem, p_sem, own_sem,
 ):
     n_gx, n_gy, n_f, n_l, tx, ty, modes = dims
     n_j = n_gx // 2
@@ -69,7 +72,7 @@
     kz = 2 * kyb
     rows = n_l * n_fh * kb
     n_t = rt.shape[1]
-    chunks = chunk_levels(n_l)
+    off_plane, off_z = offsets(n_p, n_z)
     gx = lax.axis_index("gx")
     gy = lax.axis_index("gy")
     core = lax.rem(gx, 2)
@@ -78,6 +81,10 @@
     partner = 2 * chip + other
     z, y_lo = lax.div(gy, 2), lax.rem(gy, 2)
     plane = 2 * chip + y_lo
+    p_x, p_y = lax.div(plane, 4), lax.rem(plane, 4)
+
+    def mate(o):
+        return 4 * lax.rem(p_x + o[0], n_p // 4) + lax.rem(p_y + o[1], 4)
     up_x, dn_x = lax.rem(gx + 1, n_gx), lax.rem(gx + n_gx - 1, n_gx)
     up_y, dn_y = lax.rem(gy + 1, n_gy), lax.rem(gy + n_gy - 1, n_gy)
 
@@ -232,7 +239,7 @@
 
         return lax.fori_loop(0, tx // STRIP, strip, carry)
 
-    lax.fori_loop(0, n_l // 2, stencil, 0)
+    lax.fori_loop(0, min(1, n_l - 1), stencil, 0)
 
     pl.semaphore_wait(barrier, 6 + (n_p - 1) + (n_z - 1))
 
@@ -282,7 +289,7 @@
     for c in given:
         c.start()
 
-    lax.fori_loop(n_l // 2, n_l, stencil, 0)
+    lax.fori_loop(min(1, n_l - 1), n_l, stencil, 0)
 
     for k in range(4):
         halo_copy(k).wait_recv()
@@ -311,25 +318,30 @@
             device_id=to_x(partner), device_id_type=MESH,
         )
 
-    def chip_copy(k, d, arrival=False):
-        l0, span = chunks[k]
-        there = lax.rem(plane + d, n_p)
-        slot = there if arrival else plane
-        return pltpu.make_async_remote_copy(
-            src_ref=mine.at[pl.ds(l0, span), there], dst_ref=chip_in.at[pl.ds(l0, span), slot],
-            send_sem=chip_send.at[k, there], recv_sem=chip_recv.at[k, slot],
+    def chip_copy(l, o):
+        there = mate(o)
+        return pltpu.make_async_remote_copy(
+            src_ref=mine.at[l, there], dst_ref=chip_in.at[l, plane],
+            send_sem=chip_send.at[l], recv_sem=chip_recv.at[l],
             device_id=to_plane(there), device_id_type=MESH,
+        )
+
+    def chip_all(l):
+        whole = pl.ds(0, n_p - 1)
+        return pltpu.make_async_remote_copy(
+            src_ref=mine.at[l, whole], dst_ref=chip_in.at[l, whole],
+            send_sem=chip_send.at[l], recv_sem=chip_recv.at[l],
+            device_id=to_plane(mate(off_plane[0])), device_id_type=MESH,
         )
 
     def out_copy(l):
         return pltpu.make_async_copy(out_s.at[l], stepped.at[l], out_sem.at[l])
 
-    def pass_on(k):
-        l0, span = chunks[k]
-        for l in range(l0, l0 + span):
-            core_copy(l).wait_recv()
-            mine[l] = part[l, core] + core_in[l]
-        lax.fori_loop(1, n_p, lambda d, c: (chip_copy(k, d).start(), c)[1], 0)
+    def pass_on(l):
+        core_copy(l).wait_recv()
+        mine[l] = part[l, core] + core_in[l]
+        for o in off_plane:
+            chip_copy(l, o).start()
 
     def level(l, carry):
         for f in range(n_f):
@@ -353,115 +365,125 @@
                         value = value + jnp.where(is_last, top, 0.0)
                     if h in (0, n_h - 1):
                         out_s[l, f, here, lanes] = value
-                    hi_s[f, here, lanes], lo_s[f, here, lanes] = split(value)
+                    wide = pl.ds(f * ty + h * 128, 128)
+                    hi_s[here, wide], lo_s[here, wide] = split(value)
             return c
 
         lax.fori_loop(0, tx // STRIP, strip, 0)
         out_copy(l).start()
-        both = dot(hi_s[...].reshape(n_f * tx, ty), ey_s[...])
-        left = both[:, :modes] + both[:, modes:]
-        left = left + dot(lo_s[...].reshape(n_f * tx, ty), ey_s[:, :modes])
+        both = dot(ex_s[...], hi_s[...])
+        left = both[:modes] + both[modes:] + dot(ex_s[:modes, :], lo_s[...])
         left_hi, left_lo = split(left)
 
-        def beside(v):
-            return jnp.concatenate([v[f * tx : (f + 1) * tx] for f in range(n_f)], axis=1)
-
-        both = dot(ex_s[...], beside(left_hi))
-        proj = both[:modes] + both[modes:] + dot(ex_s[:modes, :], beside(left_lo))
+        def below(v):
+            return jnp.concatenate([v[:, f * ty : (f + 1) * ty] for f in range(n_f)], axis=0)
+
+        both = dot(below(left_hi), ey_s[...])
+        proj = both[:, :modes] + both[:, modes:] + dot(below(left_lo), ey_s[:, :modes])
         for g in range(n_gx):
             for f in range(n_f):
-                part[l, g % 2, 2 * (g // 2) + f // n_fh, f % n_fh] = proj[
-                    g * kb : (g + 1) * kb, f * modes : (f + 1) * modes
-                ]
+                at = f * modes + g * kb
+                part[l, g % 2, 2 * (g // 2) + f // n_fh, f % n_fh] = proj[at : at + kb]
         core_copy(l).start()
 
-        for k in range(len(chunks) - 1):
-            pl.when(l == sum(chunks[k]))(functools.partial(pass_on, k))
+        @pl.when(l > 0)
+        def _():
+            pass_on(l - 1)
 
         return carry
 
     lax.fori_loop(0, n_l, level, 0)
-    pass_on(len(chunks) - 1)
-
-    for k, (l0, span) in enumerate(chunks):
-
-        def add(d, t, k=k, l0=l0, span=span):
-            chip_copy(k, d, True).wait_recv()
-            return t + chip_in[l0 : l0 + span, lax.rem(plane + d, n_p)]
-
-        total = lax.fori_loop(1, n_p, add, mine[l0 : l0 + span, plane])
-        row_s[l0 * n_fh * kb : (l0 + span) * n_fh * kb, :] = total.reshape(span * n_fh * kb, 128)
+    pass_on(n_l - 1)
+
+    def sum_level(l, carry):
+        chip_all(l).wait_recv()
+        chip_in[l, plane] = mine[l, plane]
+        total = chip_in[l, 0]
+        for q in range(1, n_p):
+            total = total + chip_in[l, q]
+        some = n_fh * kb
+        row_s[pl.ds(pl.multiple_of(l * some, some), some), :] = total.reshape(some, 128)
+        return carry
+
+    lax.fori_loop(0, n_l, sum_level, 0)
     for t in range(n_t):
         rt[:, t] = row_s[t * 128 : (t + 1) * 128, :].T.reshape(n_z, kz, 128)
 
-    def z_copy(d, arrival=False):
+    next_z = to_z(lax.rem(z + 1, n_z))
+
+    def z_copy(d):
         there = lax.rem(z + d, n_z)
-        slot = there if arrival else z
-        return pltpu.make_async_remote_copy(
-            src_ref=rt.at[there], dst_ref=z_in.at[slot],
-            send_sem=z_send.at[there], recv_sem=z_recv.at[slot],
+        return pltpu.make_async_remote_copy(
+            src_ref=rt.at[there], dst_ref=z_in.at[z], send_sem=z_sem.at[0], recv_sem=z_sem.at[1],
             device_id=to_z(there), device_id_type=MESH,
         )
 
-    lax.fori_loop(1, n_z, lambda d, c: (z_copy(d).start(), c)[1], 0)
+    def g_copy(d):
+        there = lax.rem(z + d, n_z)
+        return pltpu.make_async_remote_copy(
+            src_ref=gt.at[z], dst_ref=gt.at[z], send_sem=z_sem.at[2], recv_sem=z_sem.at[3],
+            device_id=to_z(there), device_id_type=MESH,
+        )
+
+    def z_all(ref, k):
+        some = ref.at[pl.ds(0, n_z - 1)]
+        return pltpu.make_async_remote_copy(
+            src_ref=some, dst_ref=some, send_sem=z_sem.at[k], recv_sem=z_sem.at[k + 1],
+            device_id=next_z, device_id_type=MESH,
+        )
+
+    for d in off_z:
+        z_copy(d).start()
     parent_copy.wait_recv()
-    target = jnp.concatenate([pt[0], pt[1]], axis=1)
-
-    def z_add(d, t):
-        z_copy(d, True).wait_recv()
-        return t + z_in[lax.rem(z + d, n_z)]
-
-    total = lax.fori_loop(1, n_z, z_add, rt[z])
-    gt[z] = target - total
-
-    def g_copy(d, arrival=False):
-        there = lax.rem(z + d, n_z)
-        slot = there if arrival else z
-        return pltpu.make_async_remote_copy(
-            src_ref=gt.at[z], dst_ref=gt.at[slot],
-            send_sem=g_send.at[there], recv_sem=g_recv.at[slot],
-            device_id=to_z(there), device_id_type=MESH,
-        )
-
-    lax.fori_loop(1, n_z, lambda d, c: (g_copy(d).start(), c)[1], 0)
-    lax.fori_loop(1, n_z, lambda d, c: (g_copy(d, True).wait_recv(), c)[1], 0)
+    z_all(z_in, 0).wait_recv()
+    z_in[z] = rt[z]
+    total = z_in[0]
+    for i in range(1, n_z):
+        total = total + z_in[i]
+    gt[z] = jnp.concatenate([pt[0], pt[1]], axis=1) - total
+    for d in off_z:
+        g_copy(d).start()
+    z_all(gt, 2).wait_recv()
     for t in range(n_t):
         blk[t * 128 : (t + 1) * 128, :] = gt[:, t].reshape(128, 128).T
 
     block = blk.at[pl.ds(0, rows), :]
 
     def place(q, c):
-        return gap.at[2 * lax.div(q, 2) + c, lax.rem(q, 2)]
-
-    def b_copy(d, arrival=False):
-        there = lax.rem(plane + d, n_p)
+        return gap.at[4 * lax.div(q, 2) + 2 * c + lax.rem(q, 2)]
+
+    def b_copy(o, arrival=False):
+        there = mate(o)
         slot = there if arrival else plane
         return pltpu.make_async_remote_copy(
             src_ref=block, dst_ref=place(slot, core),
-            send_sem=b_send.at[there], recv_sem=b_recv.at[slot],
+            send_sem=b_send, recv_sem=b_recv.at[slot],
             device_id=to_plane(there), device_id_type=MESH,
         )
 
-    def f_copy(q, src=None, arrival=False):
-        at = place(q, other if arrival else core)
+    def f_copy(q, src=None):
+        at = place(q, core)
         return pltpu.make_async_remote_copy(
             src_ref=at if src is None else src, dst_ref=at,
-            send_sem=f_send.at[q], recv_sem=f_recv.at[q],
+            send_sem=f_sem.at[0], recv_sem=f_sem.at[1],
             device_id=to_x(partner), device_id_type=MESH,
         )
 
-    lax.fori_loop(1, n_p, lambda d, c: (b_copy(d).start(), c)[1], 0)
+    for o in off_plane:
+        b_copy(o).start()
     f_copy(plane, block).start()
     own = pltpu.make_async_copy(block, place(plane, core), own_sem.at[0])
     own.start()
 
-    def forward(d, c):
-        b_copy(d, True).wait_recv()
-        f_copy(lax.rem(plane + d, n_p)).start()
-        return c
-
-    lax.fori_loop(1, n_p, forward, 0)
-    lax.fori_loop(0, n_p, lambda q, c: (f_copy(q, None, True).wait_recv(), c)[1], 0)
+    for o in off_plane:
+        b_copy(o, True).wait_recv()
+        f_copy(mate(o)).start()
+    f_all = pltpu.make_async_remote_copy(
+        src_ref=gap.at[pl.ds(0, n_p)], dst_ref=gap.at[pl.ds(0, n_p)],
+        send_sem=f_sem.at[0], recv_sem=f_sem.at[1],
+        device_id=to_x(partner), device_id_type=MESH,
+    )
+    f_all.wait_recv()
 
     own.wait()
     for c in given:
@@ -477,22 +499,15 @@
 
     lax.fori_loop(0, n_l, drain, 0)
 
-    def drain_plane(d, c):
-        for k in range(len(chunks)):
-            chip_copy(k, d).wait_send()
-        b_copy(d).wait_send()
-        f_copy(lax.rem(plane + d, n_p)).wait_send()
-        return c
-
-    lax.fori_loop(1, n_p, drain_plane, 0)
-    f_copy(plane, block).wait_send()
-
-    def drain_z(d, c):
-        z_copy(d).wait_send()
-        g_copy(d).wait_send()
-        return c
-
-    lax.fori_loop(1, n_z, drain_z, 0)
+    lax.fori_loop(0, n_l, lambda l, c: (chip_all(l).wait_send(), c)[1], 0)
+    z_all(z_in, 0).wait_send()
+    z_all(gt, 2).wait_send()
+    pltpu.make_async_remote_copy(
+        src_ref=gap.at[pl.ds(0, n_p - 1)], dst_ref=gap.at[pl.ds(0, n_p - 1)],
+        send_sem=b_send, recv_sem=b_recv.at[0],
+        device_id=to_x(partner), device_id_type=MESH,
+    ).wait_send()
+    f_all.wait_send()
 
 
 def synth_kernel(dims, stepped, gap, sea, wide_x, tall_y, nudge, out, st, out_sem):
@@ -506,7 +521,13 @@
     def level(l, carry):
         g = jnp.concatenate(
             [
-                gap[:, f // n_fh, pl.ds((l * n_fh + f % n_fh) * kb, kb), :].reshape(modes, modes)
+                jnp.concatenate(
+                    [
+                        gap[2 * i + f // n_fh, pl.ds((l * n_fh + f % n_fh) * kb, kb), :]
+                        for i in range(n_gx)
+                    ],
+                    axis=0,
+                )
                 for f in range(n_f)
             ],
             axis=1,
@@ -536,7 +557,6 @@
     rows = n_l * n_fh * kb
     n_t = -(-rows // 128)
     n_z, n_p, kz = n_gy // 2, n_gx, 2 * kyb
-    n_k = len(chunk_levels(n_l))
     n_j = n_gx // 2
     n_h = ty // 128
     dims = (n_gx, n_gy, n_f, n_l, tx, ty, modes)
@@ -555,7 +575,7 @@
         functools.partial(step_kernel, dims),
         out_shape=(
             pltpu.VMEM((n_l, n_f, tx, ty), f32),
-            pltpu.VMEM((n_gx, 2, rows, 128), f32),
+            pltpu.VMEM((2 * n_gx, rows, 128), f32),
             pltpu.VMEM((tx, ty), f32),
             pltpu.VMEM((tx, 2 * modes), bf16),
             pltpu.VMEM((3 * modes, ty), bf16),
@@ -579,8 +599,8 @@
             pltpu.VMEM((3 * modes, ty), bf16),
             pltpu.VMEM((6, n_h, tx, 128), f32),
             pltpu.VMEM((n_l, n_f, tx, ty), f32),
-            pltpu.VMEM((n_f, tx, ty), bf16),
-            pltpu.VMEM((n_f, tx, ty), bf16),
+            pltpu.VMEM((tx, n_f * ty), bf16),
+            pltpu.VMEM((tx, n_f * ty), bf16),
             pltpu.VMEM((2, HALO, ty), f32),
             pltpu.VMEM((2, HALO, ty), f32),
             pltpu.VMEM((2, HALO, tx), f32),
@@ -600,9 +620,8 @@
             pltpu.VMEM((n_z, n_t, kz, 128), f32),
             pltpu.VMEM((n_t * 128, 128), f32),
             dma((n_l, n_h)), dma((8,)), dma((4,)), dma((4,)), dma((n_l,)),
-            dma((n_l,)), dma((n_l,)), dma((n_k, n_p)), dma((n_k, n_p)),
-            dma((n_z,)), dma((n_z,)), dma((n_z,)), dma((n_z,)),
-            dma((n_p,)), dma((n_p,)), dma((n_p,)), dma((n_p,)), dma((2,)), dma((4,)),
+            dma((n_l,)), dma((n_l,)), dma((n_l,)), dma((n_l,)), dma((4,)),
+            dma, dma((n_p,)), dma((2,)), dma((2,)), dma((4,)),
         ],
         compiler_params=pltpu.CompilerParams(
             collective_id=0, has_side_effects=True, vmem_limit_bytes=46 * 2**20

time: 59.2 us -> 54 us (0.912)
  Pallas kernels: 59.1 us -> 53.9 us
    pallas_call x1, Pallas kernels: 54.1 us -> 48.9 us  [body(): pl.pallas_call(functools.partial(step_kernel, dims), out_shape=(pltpu.VME...]
where the time goes in v4:
time: 54 us; the launch traced here: 53.9 us
  Pallas kernels  53.9 us (100%)
    pallas_call x1, Pallas kernels, body(): pl.pallas_call(functools.partial(step_kernel, dims), out_shape=(pltpu.VME...  48.9 us
    pallas_call x1, Pallas kernels, body(): pl.pallas_call(functools.partial(synth_kernel, dims), out_shape=jax.Shape...  5 us

profile of v4, /device:TPU:1, one launch (start us, length us, event | category | flops | bytes accessed | tf_op | source)
XLA Modules:
  0.0 53.9 jit_solution(1137467925794188585)
XLA Ops:
  0.0 0.0 copy-start
  0.0 48.9 %step_and_project.1 = (f32[5,4,256,256]{3,2,1,0:T(8,128)S(1)}, f32[32,80,128]{2,1,0:T(8,128)S(1)}, f32[256,256]{1,0:T(8,128)S(1)}, bf16[256,256]{1,0:T(8,128)(2,1)S(1)}, bf16[384,256]{1,0:T(8,128)(2,1)S(1)}) custom-call(f32[4,5,256,256]{3,2,1,0:T(8,128)} %fields.1, s32[256,256]{1,0:T(8,128)} %mask.1, f32[256,256]{1,0:T(8,128)} %diff.1, f32[256,256]{1,0:T(8,128)} %cor.1, ...), custom_call_target="tpu_custom_call" | custom-call | tf_op jit(solution)/shard_map/step_and_project/pallas_call | solution.py:574
  48.9 0.0 copy-done
  48.9 5.0 %synthesis.1 = f32[4,5,256,256]{3,2,1,0:T(8,128)} custom-call(f32[5,4,256,256]{3,2,1,0:T(8,128)S(1)} %get-tuple-element.10.stepped, f32[32,80,128]{2,1,0:T(8,128)S(1)} %get-tuple-element.11.gap, f32[256,256]{1,0:T(8,128)S(1)} %get-tuple-element.12.sea, bf16[256,256]{1,0:T(8,128)(2,1)S(1)} %get-tuple-element.13.wide_x, ...), custom_call_target="tpu_custom_call" | custom-call | tf_op jit(solution)/shard_map/synthesis/pallas_call | solution.py:632
Async XLA Ops:
  0.0 48.9 %copy-start = (f32[4,5]{1,0:T(4,128)S(1)}, f32[4,5]{1,0:T(4,128)}, u32[]{:S(2)}) copy-start(f32[4,5]{1,0:T(4,128)} %nudge.1) | copy-start | bytes 244

commit v5 on v4

--- a/solution.py
+++ b/solution.py
@@ -36,6 +36,11 @@
     plane.sort(key=lambda o: -(min(o[0], n_x - o[0]) + min(o[1], n_y - o[1])))
     line = sorted(range(1, n_z), key=lambda d: -min(d, n_z - d))
     return plane, line
+
+
+def level_parts(n_l):
+    first = (n_l + 1) // 2
+    return [(0, first), (first, n_l - first)]
 
 
 def split(value):
@@ -58,7 +63,7 @@
     part, core_in, mine, chip_in, row_s, rt, z_in, pth, pt, gt, blk,
     in_sem, tab_sem, halo_send, halo_recv, out_sem,
     core_send, core_recv, chip_send, chip_recv, z_sem,
-    b_send, b_recv, f_sem, p_sem, own_sem,
+    b_send, b_recv, f_sem, blk_sem, p_sem, own_sem,
 ):
     n_gx, n_gy, n_f, n_l, tx, ty, modes = dims
     n_j = n_gx // 2
@@ -71,8 +76,9 @@
     n_p = 2 * n_j
     kz = 2 * kyb
     rows = n_l * n_fh * kb
-    n_t = rt.shape[1]
     off_plane, off_z = offsets(n_p, n_z)
+    parts = level_parts(n_l)
+    some = n_fh * kb
     gx = lax.axis_index("gx")
     gy = lax.axis_index("gy")
     core = lax.rem(gx, 2)
@@ -260,14 +266,14 @@
 
     ey_s[:, :modes], ey_s[:, modes:] = split(yf_s[...])
     ex_s[:modes, :], ex_s[modes:, :] = split(xf_s[...])
-    pack_rows = n_t * 128
     for half in range(2):
-        blk[...] = jnp.zeros((pack_rows, 128), jnp.float32)
-        for f in range(n_fh):
-            for l in range(n_l):
-                blk[pl.ds((l * n_fh + f) * kb, kb), pl.ds(0, kyb)] = parent[half * n_fh + f, l]
-        for t in range(n_t):
-            pth[half, t] = blk[t * 128 : (t + 1) * 128, :].T[:kyb]
+        for t, (l0, span) in enumerate(parts):
+            blk[t] = jnp.zeros((128, 128), jnp.float32)
+            for f in range(n_fh):
+                for l in range(span):
+                    block = parent[half * n_fh + f, l0 + l]
+                    blk[t, pl.ds((l * n_fh + f) * kb, kb), pl.ds(0, kyb)] = block
+            pth[half, t] = blk[t].T[:kyb]
     parent_copy = pltpu.make_async_remote_copy(
         src_ref=pth.at[1 - y_lo], dst_ref=pt.at[y_lo],
         send_sem=p_sem.at[0], recv_sem=p_sem.at[1],
@@ -275,16 +281,16 @@
     )
     parent_copy.start()
     pt[y_lo] = pth[y_lo]
-    row_s[...] = jnp.zeros((pack_rows, 128), jnp.float32)
+    row_s[...] = jnp.zeros(row_s.shape, jnp.float32)
     wo_s[:, :modes], wo_s[:, modes:] = split(wf_s[...])
     t_hi, t_lo = split(tf_s[...])
     to_s[:modes, :] = t_hi
     to_s[modes : 2 * modes, :] = t_hi
     to_s[2 * modes :, :] = t_lo
     given = [
-        pltpu.make_async_copy(m_s.at[0], sea, own_sem.at[1]),
-        pltpu.make_async_copy(wo_s, wide_out, own_sem.at[2]),
-        pltpu.make_async_copy(to_s, tall_out, own_sem.at[3]),
+        pltpu.make_async_copy(m_s.at[0], sea, own_sem.at[0]),
+        pltpu.make_async_copy(wo_s, wide_out, own_sem.at[1]),
+        pltpu.make_async_copy(to_s, tall_out, own_sem.at[2]),
     ]
     for c in given:
         c.start()
@@ -395,97 +401,118 @@
     lax.fori_loop(0, n_l, level, 0)
     pass_on(n_l - 1)
 
-    def sum_level(l, carry):
-        chip_all(l).wait_recv()
-        chip_in[l, plane] = mine[l, plane]
-        total = chip_in[l, 0]
-        for q in range(1, n_p):
-            total = total + chip_in[l, q]
-        some = n_fh * kb
-        row_s[pl.ds(pl.multiple_of(l * some, some), some), :] = total.reshape(some, 128)
-        return carry
-
-    lax.fori_loop(0, n_l, sum_level, 0)
-    for t in range(n_t):
-        rt[:, t] = row_s[t * 128 : (t + 1) * 128, :].T.reshape(n_z, kz, 128)
-
     next_z = to_z(lax.rem(z + 1, n_z))
 
-    def z_copy(d):
+    def z_copy(t, d):
         there = lax.rem(z + d, n_z)
         return pltpu.make_async_remote_copy(
-            src_ref=rt.at[there], dst_ref=z_in.at[z], send_sem=z_sem.at[0], recv_sem=z_sem.at[1],
+            src_ref=rt.at[t, there], dst_ref=z_in.at[t, z],
+            send_sem=z_sem.at[t, 0], recv_sem=z_sem.at[t, 1],
             device_id=to_z(there), device_id_type=MESH,
         )
 
-    def g_copy(d):
+    def g_copy(t, d):
         there = lax.rem(z + d, n_z)
         return pltpu.make_async_remote_copy(
-            src_ref=gt.at[z], dst_ref=gt.at[z], send_sem=z_sem.at[2], recv_sem=z_sem.at[3],
+            src_ref=gt.at[t, z], dst_ref=gt.at[t, z],
+            send_sem=z_sem.at[t, 2], recv_sem=z_sem.at[t, 3],
             device_id=to_z(there), device_id_type=MESH,
         )
 
-    def z_all(ref, k):
-        some = ref.at[pl.ds(0, n_z - 1)]
-        return pltpu.make_async_remote_copy(
-            src_ref=some, dst_ref=some, send_sem=z_sem.at[k], recv_sem=z_sem.at[k + 1],
+    def z_all(ref, t, k):
+        whole = ref.at[t, pl.ds(0, n_z - 1)]
+        return pltpu.make_async_remote_copy(
+            src_ref=whole, dst_ref=whole, send_sem=z_sem.at[t, k], recv_sem=z_sem.at[t, k + 1],
             device_id=next_z, device_id_type=MESH,
         )
 
-    for d in off_z:
-        z_copy(d).start()
-    parent_copy.wait_recv()
-    z_all(z_in, 0).wait_recv()
-    z_in[z] = rt[z]
-    total = z_in[0]
-    for i in range(1, n_z):
-        total = total + z_in[i]
-    gt[z] = jnp.concatenate([pt[0], pt[1]], axis=1) - total
-    for d in off_z:
-        g_copy(d).start()
-    z_all(gt, 2).wait_recv()
-    for t in range(n_t):
-        blk[t * 128 : (t + 1) * 128, :] = gt[:, t].reshape(128, 128).T
-
-    block = blk.at[pl.ds(0, rows), :]
-
-    def place(q, c):
-        return gap.at[4 * lax.div(q, 2) + 2 * c + lax.rem(q, 2)]
-
-    def b_copy(o, arrival=False):
+    def rows_of(t):
+        l0, span = parts[t]
+        return pl.ds(l0 * some, span * some)
+
+    def place(q, c, t):
+        return gap.at[4 * lax.div(q, 2) + 2 * c + lax.rem(q, 2), rows_of(t)]
+
+    def block(t):
+        return blk.at[t, pl.ds(0, parts[t][1] * some)]
+
+    def b_copy(t, o, arrival=False):
         there = mate(o)
         slot = there if arrival else plane
         return pltpu.make_async_remote_copy(
-            src_ref=block, dst_ref=place(slot, core),
-            send_sem=b_send, recv_sem=b_recv.at[slot],
+            src_ref=block(t), dst_ref=place(slot, core, t),
+            send_sem=b_send.at[t], recv_sem=b_recv.at[t, slot],
             device_id=to_plane(there), device_id_type=MESH,
         )
 
-    def f_copy(q, src=None):
-        at = place(q, core)
+    def f_copy(t, q, src=None):
+        at = place(q, core, t)
         return pltpu.make_async_remote_copy(
             src_ref=at if src is None else src, dst_ref=at,
-            send_sem=f_sem.at[0], recv_sem=f_sem.at[1],
+            send_sem=f_sem.at[t, 0], recv_sem=f_sem.at[t, 1],
             device_id=to_x(partner), device_id_type=MESH,
         )
 
-    for o in off_plane:
-        b_copy(o).start()
-    f_copy(plane, block).start()
-    own = pltpu.make_async_copy(block, place(plane, core), own_sem.at[0])
-    own.start()
-
-    for o in off_plane:
-        b_copy(o, True).wait_recv()
-        f_copy(mate(o)).start()
-    f_all = pltpu.make_async_remote_copy(
-        src_ref=gap.at[pl.ds(0, n_p)], dst_ref=gap.at[pl.ds(0, n_p)],
-        send_sem=f_sem.at[0], recv_sem=f_sem.at[1],
-        device_id=to_x(partner), device_id_type=MESH,
-    )
-    f_all.wait_recv()
-
-    own.wait()
+    def own_copy(t):
+        return pltpu.make_async_copy(block(t), place(plane, core, t), blk_sem.at[t])
+
+    def sum_plane(t):
+        l0, span = parts[t]
+        for l in range(l0, l0 + span):
+            chip_all(l).wait_recv()
+            chip_in[l, plane] = mine[l, plane]
+            total = chip_in[l, 0]
+            for q in range(1, n_p):
+                total = total + chip_in[l, q]
+            row_s[t, (l - l0) * some : (l - l0 + 1) * some, :] = total.reshape(some, 128)
+        rt[t] = row_s[t].T.reshape(n_z, kz, 128)
+        for d in off_z:
+            z_copy(t, d).start()
+
+    def sum_z(t):
+        z_all(z_in, t, 0).wait_recv()
+        z_in[t, z] = rt[t, z]
+        total = z_in[t, 0]
+        for i in range(1, n_z):
+            total = total + z_in[t, i]
+        gt[t, z] = jnp.concatenate([pt[0, t], pt[1, t]], axis=0) - total
+        for d in off_z:
+            g_copy(t, d).start()
+
+    def spread(t):
+        z_all(gt, t, 2).wait_recv()
+        blk[t] = gt[t].reshape(128, 128).T
+        for o in off_plane:
+            b_copy(t, o).start()
+        f_copy(t, plane, block(t)).start()
+        own_copy(t).start()
+
+    def forward(t):
+        for o in off_plane:
+            b_copy(t, o, True).wait_recv()
+            f_copy(t, mate(o)).start()
+
+    def all_of(t, count, send, recv):
+        whole = gap.at[pl.ds(0, count), rows_of(t)]
+        return pltpu.make_async_remote_copy(
+            src_ref=whole, dst_ref=whole, send_sem=send, recv_sem=recv,
+            device_id=to_x(partner), device_id_type=MESH,
+        )
+
+    n_t = len(parts)
+    for t in range(n_t):
+        sum_plane(t)
+        if t == 0:
+            parent_copy.wait_recv()
+    for t in range(n_t):
+        sum_z(t)
+    for t in range(n_t):
+        spread(t)
+    for t in range(n_t):
+        forward(t)
+    for t in range(n_t):
+        all_of(t, n_p, f_sem.at[t, 0], f_sem.at[t, 1]).wait_recv()
+
     for c in given:
         c.wait()
     parent_copy.wait_send()
@@ -500,14 +527,12 @@
     lax.fori_loop(0, n_l, drain, 0)
 
     lax.fori_loop(0, n_l, lambda l, c: (chip_all(l).wait_send(), c)[1], 0)
-    z_all(z_in, 0).wait_send()
-    z_all(gt, 2).wait_send()
-    pltpu.make_async_remote_copy(
-        src_ref=gap.at[pl.ds(0, n_p - 1)], dst_ref=gap.at[pl.ds(0, n_p - 1)],
-        send_sem=b_send, recv_sem=b_recv.at[0],
-        device_id=to_x(partner), device_id_type=MESH,
-    ).wait_send()
-    f_all.wait_send()
+    for t in range(n_t):
+        own_copy(t).wait()
+        z_all(z_in, t, 0).wait_send()
+        z_all(gt, t, 2).wait_send()
+        all_of(t, n_p - 1, b_send.at[t], b_recv.at[t, 0]).wait_send()
+        all_of(t, n_p, f_sem.at[t, 0], f_sem.at[t, 1]).wait_send()
 
 
 def synth_kernel(dims, stepped, gap, sea, wide_x, tall_y, nudge, out, st, out_sem):
@@ -555,7 +580,7 @@
     kb, kyb = modes // n_gx, modes // n_gy
     n_fh = n_f // 2
     rows = n_l * n_fh * kb
-    n_t = -(-rows // 128)
+    n_t = len(level_parts(n_l))
     n_z, n_p, kz = n_gy // 2, n_gx, 2 * kyb
     n_j = n_gx // 2
     n_h = ty // 128
@@ -612,16 +637,16 @@
             pltpu.VMEM((n_l, n_p, n_fh, kb, 128), f32),
             pltpu.VMEM((n_l, n_p, n_fh, kb, 128), f32),
             pltpu.VMEM((n_l, n_p, n_fh, kb, 128), f32),
-            pltpu.VMEM((n_t * 128, 128), f32),
-            pltpu.VMEM((n_z, n_t, kz, 128), f32),
-            pltpu.VMEM((n_z, n_t, kz, 128), f32),
+            pltpu.VMEM((n_t, 128, 128), f32),
+            pltpu.VMEM((n_t, n_z, kz, 128), f32),
+            pltpu.VMEM((n_t, n_z, kz, 128), f32),
             pltpu.VMEM((2, n_t, kyb, 128), f32),
             pltpu.VMEM((2, n_t, kyb, 128), f32),
-            pltpu.VMEM((n_z, n_t, kz, 128), f32),
-            pltpu.VMEM((n_t * 128, 128), f32),
+            pltpu.VMEM((n_t, n_z, kz, 128), f32),
+            pltpu.VMEM((n_t, 128, 128), f32),
             dma((n_l, n_h)), dma((8,)), dma((4,)), dma((4,)), dma((n_l,)),
-            dma((n_l,)), dma((n_l,)), dma((n_l,)), dma((n_l,)), dma((4,)),
-            dma, dma((n_p,)), dma((2,)), dma((2,)), dma((4,)),
+            dma((n_l,)), dma((n_l,)), dma((n_l,)), dma((n_l,)), dma((n_t, 4)),
+            dma((n_t,)), dma((n_t, n_p)), dma((n_t, 2)), dma((n_t,)), dma((2,)), dma((3,)),
         ],
         compiler_params=pltpu.CompilerParams(
             collective_id=0, has_side_effects=True, vmem_limit_bytes=46 * 2**20

time: 54 us -> 52 us (0.963)
  Pallas kernels: 53.9 us -> 51.9 us
    pallas_call x1, Pallas kernels: 48.9 us -> 46.9 us  [body(): pl.pallas_call(functools.partial(step_kernel, dims), out_shape=(pltpu.VME...]
where the time goes in v5:
time: 52 us; the launch traced here: 51.9 us
  Pallas kernels  51.9 us (100%)
    pallas_call x1, Pallas kernels, body(): pl.pallas_call(functools.partial(step_kernel, dims), out_shape=(pltpu.VME...  46.9 us
    pallas_call x1, Pallas kernels, body(): pl.pallas_call(functools.partial(synth_kernel, dims), out_shape=jax.Shape...  5.01 us

profile of v5, /device:TPU:1, one launch (start us, length us, event | category | flops | bytes accessed | tf_op | source)
XLA Modules:
  0.0 51.9 jit_solution(15132798483601267329)
XLA Ops:
  0.0 0.0 copy-start
  0.0 46.9 %step_and_project.1 = (f32[5,4,256,256]{3,2,1,0:T(8,128)S(1)}, f32[32,80,128]{2,1,0:T(8,128)S(1)}, f32[256,256]{1,0:T(8,128)S(1)}, bf16[256,256]{1,0:T(8,128)(2,1)S(1)}, bf16[384,256]{1,0:T(8,128)(2,1)S(1)}) custom-call(f32[4,5,256,256]{3,2,1,0:T(8,128)} %fields.1, s32[256,256]{1,0:T(8,128)} %mask.1, f32[256,256]{1,0:T(8,128)} %diff.1, f32[256,256]{1,0:T(8,128)} %cor.1, ...), custom_call_target="tpu_custom_call" | custom-call | tf_op jit(solution)/shard_map/step_and_project/pallas_call | solution.py:599
  46.9 0.0 copy-done
  46.9 5.0 %synthesis.1 = f32[4,5,256,256]{3,2,1,0:T(8,128)} custom-call(f32[5,4,256,256]{3,2,1,0:T(8,128)S(1)} %get-tuple-element.10.stepped, f32[32,80,128]{2,1,0:T(8,128)S(1)} %get-tuple-element.11.gap, f32[256,256]{1,0:T(8,128)S(1)} %get-tuple-element.12.sea, bf16[256,256]{1,0:T(8,128)(2,1)S(1)} %get-tuple-element.13.wide_x, ...), custom_call_target="tpu_custom_call" | custom-call | tf_op jit(solution)/shard_map/synthesis/pallas_call | solution.py:657
Async XLA Ops:
  0.0 46.9 %copy-start = (f32[4,5]{1,0:T(4,128)S(1)}, f32[4,5]{1,0:T(4,128)}, u32[]{:S(2)}) copy-start(f32[4,5]{1,0:T(4,128)} %nudge.1) | copy-start | bytes 244

commit v6 on v5

--- a/solution.py
+++ b/solution.py
@@ -55,12 +55,12 @@
 
 def step_kernel(
     dims,
-    fields, mask, diff, cor, parent_in, wide_y, tall_x, wide_x, tall_y,
+    fields, mask, diff, cor, parent_in, wide_y, tall_x, wide_x, tall_y, nudge_in,
     stepped, gap, sea, wide_out, tall_out,
-    parent, q_s, m_s, mi_s, di_s, co_s, yf_s, xf_s, wf_s, tf_s, ey_s, ex_s, wo_s, to_s,
+    nudge, parent, q_s, m_s, mi_s, di_s, co_s, yf_s, xf_s, wf_s, tf_s, ey_s, ex_s, wo_s, to_s,
     coef, out_s, hi_s, lo_s,
     rp, rh, cp, ch, pack, hc, fix_row,
-    part, core_in, mine, chip_in, row_s, rt, z_in, pth, pt, gt, blk,
+    part, core_in, mine, chip_in, row_s, rt, z_in, pth, pt, gt, blk, gap_s,
     in_sem, tab_sem, halo_send, halo_recv, out_sem,
     core_send, core_recv, chip_send, chip_recv, z_sem,
     b_send, b_recv, f_sem, blk_sem, p_sem, own_sem,
@@ -75,7 +75,6 @@
     n_z = n_gy // 2
     n_p = 2 * n_j
     kz = 2 * kyb
-    rows = n_l * n_fh * kb
     off_plane, off_z = offsets(n_p, n_z)
     parts = level_parts(n_l)
     some = n_fh * kb
@@ -124,6 +123,7 @@
         pltpu.make_async_copy(wide_x.at[gx], wf_s, tab_sem.at[5]),
         pltpu.make_async_copy(tall_y.at[gy], tf_s, tab_sem.at[6]),
         pltpu.make_async_copy(parent_in, parent, tab_sem.at[7]),
+        pltpu.make_async_copy(nudge_in, nudge, tab_sem.at[8]),
     ]
     for c in small[:2]:
         c.start()
@@ -376,7 +376,7 @@
             return c
 
         lax.fori_loop(0, tx // STRIP, strip, 0)
-        out_copy(l).start()
+        pl.when(l >= parts[0][1])(lambda: out_copy(l).start())
         both = dot(ex_s[...], hi_s[...])
         left = both[:modes] + both[modes:] + dot(ex_s[:modes, :], lo_s[...])
         left_hi, left_lo = split(left)
@@ -426,12 +426,8 @@
             device_id=next_z, device_id_type=MESH,
         )
 
-    def rows_of(t):
-        l0, span = parts[t]
-        return pl.ds(l0 * some, span * some)
-
     def place(q, c, t):
-        return gap.at[4 * lax.div(q, 2) + 2 * c + lax.rem(q, 2), rows_of(t)]
+        return (gap_s, gap)[t].at[4 * lax.div(q, 2) + 2 * c + lax.rem(q, 2)]
 
     def block(t):
         return blk.at[t, pl.ds(0, parts[t][1] * some)]
@@ -493,7 +489,7 @@
             f_copy(t, mate(o)).start()
 
     def all_of(t, count, send, recv):
-        whole = gap.at[pl.ds(0, count), rows_of(t)]
+        whole = (gap_s, gap)[t].at[pl.ds(0, count)]
         return pltpu.make_async_remote_copy(
             src_ref=whole, dst_ref=whole, send_sem=send, recv_sem=recv,
             device_id=to_x(partner), device_id_type=MESH,
@@ -508,11 +504,26 @@
         sum_z(t)
     for t in range(n_t):
         spread(t)
-    for t in range(n_t):
-        forward(t)
-    for t in range(n_t):
-        all_of(t, n_p, f_sem.at[t, 0], f_sem.at[t, 1]).wait_recv()
-
+    def correct(l, carry):
+        corr = corrections(
+            lambda i, f: gap_s[2 * i + f // n_fh, pl.ds((l * n_fh + f % n_fh) * kb, kb), :],
+            wo_s, to_s, n_gx, n_f, modes,
+        )
+        for f in range(n_f):
+            out_s[l, f] = out_s[l, f] + (nudge[f, l] * m_s[0]) * corr(f)
+        out_copy(l).start()
+        return carry
+
+    n_first = parts[0][1]
+    forward(0)
+    all_of(0, n_p, f_sem.at[0, 0], f_sem.at[0, 1]).wait_recv()
+    own_copy(0).wait()
+    lax.fori_loop(0, 1, correct, 0)
+    forward(1)
+    lax.fori_loop(1, n_first, correct, 0)
+    all_of(1, n_p, f_sem.at[1, 0], f_sem.at[1, 1]).wait_recv()
+
+    own_copy(1).wait()
     for c in given:
         c.wait()
     parent_copy.wait_send()
@@ -528,50 +539,62 @@
 
     lax.fori_loop(0, n_l, lambda l, c: (chip_all(l).wait_send(), c)[1], 0)
     for t in range(n_t):
-        own_copy(t).wait()
         z_all(z_in, t, 0).wait_send()
         z_all(gt, t, 2).wait_send()
         all_of(t, n_p - 1, b_send.at[t], b_recv.at[t, 0]).wait_send()
         all_of(t, n_p, f_sem.at[t, 0], f_sem.at[t, 1]).wait_send()
 
 
+def corrections(block, wide, tall, n_gx, n_f, modes):
+    g = jnp.concatenate(
+        [
+            jnp.concatenate([block(i, f) for i in range(n_gx)], axis=0) for f in range(n_f)
+        ],
+        axis=1,
+    )
+    g_hi, g_lo = split(g)
+    t = dot(wide[...], jnp.concatenate([g_hi, g_hi], axis=0))
+    t_hi, t_lo = split(t + dot(wide[:, :modes], g_lo))
+
+    def of_field(f):
+        here = slice(f * modes, (f + 1) * modes)
+        both = jnp.concatenate([t_hi[:, here], t_lo[:, here]], axis=1)
+        return dot(both, tall[: 2 * modes, :]) + dot(t_hi[:, here], tall[2 * modes :, :])
+
+    return of_field
+
+
 def synth_kernel(dims, stepped, gap, sea, wide_x, tall_y, nudge, out, st, out_sem):
     n_gx, n_gy, n_f, n_l, tx, ty, modes = dims
     kb = modes // n_gx
     n_fh = n_f // 2
+    l0, span = level_parts(n_l)[1]
+
+    def ready(l, f):
+        return pltpu.make_async_copy(stepped.at[l, f], out.at[f, l], out_sem.at[l, f])
 
     def store(l, f):
-        return pltpu.make_async_copy(st.at[l, f], out.at[f, l], out_sem.at[l, f])
+        return pltpu.make_async_copy(st.at[l - l0, f], out.at[f, l], out_sem.at[l, f])
+
+    for l in range(l0):
+        for f in range(n_f):
+            ready(l, f).start()
 
     def level(l, carry):
-        g = jnp.concatenate(
-            [
-                jnp.concatenate(
-                    [
-                        gap[2 * i + f // n_fh, pl.ds((l * n_fh + f % n_fh) * kb, kb), :]
-                        for i in range(n_gx)
-                    ],
-                    axis=0,
-                )
-                for f in range(n_f)
-            ],
-            axis=1,
-        )
-        g_hi, g_lo = split(g)
-        t = dot(wide_x[...], jnp.concatenate([g_hi, g_hi], axis=0))
-        t_hi, t_lo = split(t + dot(wide_x[:, :modes], g_lo))
+        row = (l - l0) * n_fh
+        corr = corrections(
+            lambda i, f: gap[2 * i + f // n_fh, pl.ds((row + f % n_fh) * kb, kb), :],
+            wide_x, tall_y, n_gx, n_f, modes,
+        )
         for f in range(n_f):
-            here = slice(f * modes, (f + 1) * modes)
-            both = jnp.concatenate([t_hi[:, here], t_lo[:, here]], axis=1)
-            corr = dot(both, tall_y[: 2 * modes, :]) + dot(t_hi[:, here], tall_y[2 * modes :, :])
-            st[l, f] = stepped[l, f] + (nudge[f, l] * sea[...]) * corr
+            st[l - l0, f] = stepped[l, f] + (nudge[f, l] * sea[...]) * corr(f)
             store(l, f).start()
         return carry
 
-    lax.fori_loop(0, n_l, level, 0)
+    lax.fori_loop(l0, n_l, level, 0)
     for l in range(n_l):
         for f in range(n_f):
-            store(l, f).wait()
+            (ready if l < l0 else store)(l, f).wait()
 
 
 def body(n_gx, n_gy, fields, sea_mask, diffusivity, coriolis, nudge_weight, parent_modes):
@@ -579,8 +602,8 @@
     modes = parent_modes.shape[2] * n_gx
     kb, kyb = modes // n_gx, modes // n_gy
     n_fh = n_f // 2
-    rows = n_l * n_fh * kb
-    n_t = len(level_parts(n_l))
+    spans = [span for _, span in level_parts(n_l)]
+    n_t = len(spans)
     n_z, n_p, kz = n_gy // 2, n_gx, 2 * kyb
     n_j = n_gx // 2
     n_h = ty // 128
@@ -600,14 +623,15 @@
         functools.partial(step_kernel, dims),
         out_shape=(
             pltpu.VMEM((n_l, n_f, tx, ty), f32),
-            pltpu.VMEM((2 * n_gx, rows, 128), f32),
+            pltpu.VMEM((2 * n_gx, spans[1] * n_fh * kb, 128), f32),
             pltpu.VMEM((tx, ty), f32),
             pltpu.VMEM((tx, 2 * modes), bf16),
             pltpu.VMEM((3 * modes, ty), bf16),
         ),
-        in_specs=[any_space] * 9,
+        in_specs=[any_space] * 10,
         out_specs=(any_space,) * 5,
         scratch_shapes=[
+            pltpu.SMEM((n_f, n_l), f32),
             pltpu.VMEM(parent_modes.shape, f32),
             pltpu.VMEM((n_l, n_f, n_h, tx + 2 * PAD, 128), f32),
             pltpu.VMEM((2, tx, ty), f32),
@@ -644,7 +668,8 @@
             pltpu.VMEM((2, n_t, kyb, 128), f32),
             pltpu.VMEM((n_t, n_z, kz, 128), f32),
             pltpu.VMEM((n_t, 128, 128), f32),
-            dma((n_l, n_h)), dma((8,)), dma((4,)), dma((4,)), dma((n_l,)),
+            pltpu.VMEM((2 * n_gx, spans[0] * n_fh * kb, 128), f32),
+            dma((n_l, n_h)), dma((9,)), dma((4,)), dma((4,)), dma((n_l,)),
             dma((n_l,)), dma((n_l,)), dma((n_l,)), dma((n_l,)), dma((n_t, 4)),
             dma((n_t,)), dma((n_t, n_p)), dma((n_t, 2)), dma((n_t,)), dma((2,)), dma((3,)),
         ],
@@ -652,14 +677,14 @@
             collective_id=0, has_side_effects=True, vmem_limit_bytes=46 * 2**20
         ),
         name="step_and_project",
-    )(hbm(fields), hbm(sea_mask), hbm(diffusivity), hbm(coriolis), hbm(parent_modes), *tables)
+    )(hbm(fields), hbm(sea_mask), hbm(diffusivity), hbm(coriolis), hbm(parent_modes), *tables, hbm(nudge_weight))
 
     return pl.pallas_call(
         functools.partial(synth_kernel, dims),
         out_shape=jax.ShapeDtypeStruct(fields.shape, f32),
         in_specs=[vmem] * 5 + [pl.BlockSpec(memory_space=pltpu.SMEM)],
         out_specs=any_space,
-        scratch_shapes=[pltpu.VMEM((n_l, n_f, tx, ty), f32), dma((n_l, n_f))],
+        scratch_shapes=[pltpu.VMEM((spans[1], n_f, tx, ty), f32), dma((n_l, n_f))],
         compiler_params=pltpu.CompilerParams(vmem_limit_bytes=20 * 2**20),
         name="synthesis",
     )(*kept, nudge_weight)

time: 52 us -> 50.7 us (0.975)
  Pallas kernels: 51.9 us -> 50.6 us
    pallas_call x1, Pallas kernels: 5.01 us -> 3.06 us  [body(): pl.pallas_call(functools.partial(synth_kernel, dims), out_shape=jax.Shape...]
    pallas_call x1, Pallas kernels: 46.9 us -> 47.5 us  [body(): pl.pallas_call(functools.partial(step_kernel, dims), out_shape=(pltpu.VME...]
where the time goes in v6:
time: 50.7 us; the launch traced here: 50.6 us
  Pallas kernels  50.6 us (100%)
    pallas_call x1, Pallas kernels, body(): pl.pallas_call(functools.partial(step_kernel, dims), out_shape=(pltpu.VME...  47.5 us
    pallas_call x1, Pallas kernels, body(): pl.pallas_call(functools.partial(synth_kernel, dims), out_shape=jax.Shape...  3.06 us

profile of v6, /device:TPU:1, one launch (start us, length us, event | category | flops | bytes accessed | tf_op | source)
XLA Modules:
  0.0 50.6 jit_solution(17519776358986794833)
XLA Ops:
  0.0 0.0 copy-start
  0.0 47.5 %step_and_project.1 = (f32[5,4,256,256]{3,2,1,0:T(8,128)S(1)}, f32[32,32,128]{2,1,0:T(8,128)S(1)}, f32[256,256]{1,0:T(8,128)S(1)}, bf16[256,256]{1,0:T(8,128)(2,1)S(1)}, bf16[384,256]{1,0:T(8,128)(2,1)S(1)}) custom-call(f32[4,5,256,256]{3,2,1,0:T(8,128)} %fields.1, s32[256,256]{1,0:T(8,128)} %mask.1, f32[256,256]{1,0:T(8,128)} %diff.1, f32[256,256]{1,0:T(8,128)} %cor.1, ...), custom_call_target="tpu_custom_call" | custom-call | tf_op jit(solution)/shard_map/step_and_project/pallas_call | solution.py:622
  47.5 0.0 copy-done
  47.5 3.1 %synthesis.1 = f32[4,5,256,256]{3,2,1,0:T(8,128)} custom-call(f32[5,4,256,256]{3,2,1,0:T(8,128)S(1)} %get-tuple-element.10.stepped, f32[32,32,128]{2,1,0:T(8,128)S(1)} %get-tuple-element.11.gap, f32[256,256]{1,0:T(8,128)S(1)} %get-tuple-element.12.sea, bf16[256,256]{1,0:T(8,128)(2,1)S(1)} %get-tuple-element.13.wide_x, ...), custom_call_target="tpu_custom_call" | custom-call | tf_op jit(solution)/shard_map/synthesis/pallas_call | solution.py:682
Async XLA Ops:
  0.0 47.5 %copy-start = (f32[4,5]{1,0:T(4,128)S(1)}, f32[4,5]{1,0:T(4,128)}, u32[]{:S(2)}) copy-start(f32[4,5]{1,0:T(4,128)} %nudge.1) | copy-start | bytes 244

commit v7 on v6

--- a/solution.py
+++ b/solution.py
@@ -10,7 +10,7 @@
 from jax.sharding import PartitionSpec as P
 
 MESH = pl.DeviceIdType.MESH
-STRIP = 64
+STRIP = 128
 PAD = 8
 HALO = 24
 
@@ -146,8 +146,10 @@
     greet(to_y(up_y))
     greet(to_y(dn_y))
     greet(side_y)
-    lax.fori_loop(1, n_p, lambda d, c: (greet(to_plane(lax.rem(plane + d, n_p))), c)[1], 0)
-    lax.fori_loop(1, n_z, lambda d, c: (greet(to_z(lax.rem(z + d, n_z))), c)[1], 0)
+    for o in off_plane:
+        greet(to_plane(mate(o)))
+    for d in off_z:
+        greet(to_z(lax.rem(z + d, n_z)))
 
     lane = lax.broadcasted_iota(jnp.int32, (tx, 128), 1)
     for c in small[:2]:

time: 50.7 us -> 50.5 us (level)
  no operation moved by 1% of the time
where the time goes in v7:
time: 50.5 us; the launch traced here: 50.4 us
  Pallas kernels  50.4 us (100%)
    pallas_call x1, Pallas kernels, body(): pl.pallas_call(functools.partial(step_kernel, dims), out_shape=(pltpu.VME...  47.3 us
    pallas_call x1, Pallas kernels, body(): pl.pallas_call(functools.partial(synth_kernel, dims), out_shape=jax.Shape...  3.06 us

profile of v7, /device:TPU:1, one launch (start us, length us, event | category | flops | bytes accessed | tf_op | source)
XLA Modules:
  0.0 50.4 jit_solution(730922929280493966)
XLA Ops:
  0.0 0.0 copy-start
  0.0 47.3 %step_and_project.1 = (f32[5,4,256,256]{3,2,1,0:T(8,128)S(1)}, f32[32,32,128]{2,1,0:T(8,128)S(1)}, f32[256,256]{1,0:T(8,128)S(1)}, bf16[256,256]{1,0:T(8,128)(2,1)S(1)}, bf16[384,256]{1,0:T(8,128)(2,1)S(1)}) custom-call(f32[4,5,256,256]{3,2,1,0:T(8,128)} %fields.1, s32[256,256]{1,0:T(8,128)} %mask.1, f32[256,256]{1,0:T(8,128)} %diff.1, f32[256,256]{1,0:T(8,128)} %cor.1, ...), custom_call_target="tpu_custom_call" | custom-call | tf_op jit(solution)/shard_map/step_and_project/pallas_call | solution.py:624
  47.4 0.0 copy-done
  47.4 3.1 %synthesis.1 = f32[4,5,256,256]{3,2,1,0:T(8,128)} custom-call(f32[5,4,256,256]{3,2,1,0:T(8,128)S(1)} %get-tuple-element.10.stepped, f32[32,32,128]{2,1,0:T(8,128)S(1)} %get-tuple-element.11.gap, f32[256,256]{1,0:T(8,128)S(1)} %get-tuple-element.12.sea, bf16[256,256]{1,0:T(8,128)(2,1)S(1)} %get-tuple-element.13.wide_x, ...), custom_call_target="tpu_custom_call" | custom-call | tf_op jit(solution)/shard_map/synthesis/pallas_call | solution.py:684
Async XLA Ops:
  0.0 47.4 %copy-start = (f32[4,5]{1,0:T(4,128)S(1)}, f32[4,5]{1,0:T(4,128)}, u32[]{:S(2)}) copy-start(f32[4,5]{1,0:T(4,128)} %nudge.1) | copy-start | bytes 244
